TPU v7x, 32 devices: a whole 2x2x4 slice. The times are simulated.
32 devices in a mesh: pipe: 4 (over x, core), seq: 8 (over z, y).
Axes of the slice: x: 2, y: 2, z: 4, core: 2. Of those that a mesh axis runs over, the one named last changes fastest.
Arguments:
- layer_input: bfloat16 [4, 1024, 256], P('pipe', 'seq'), may hold values from -6 to 6
- filters: float32 [4, 1024, 256], P('pipe', 'seq'), may hold values from -1 to 1
- skip: float32 [4, 256], P('pipe'), may hold values from 0.5 to 1.5
- incoming: bfloat16 [4, 1024, 256], P('pipe', 'seq'), may hold values from -6 to 6
- loss_grad: bfloat16 [1024, 256], P('seq'), may hold values from -6 to 6
Outputs:
- input_grad: bfloat16 [4, 1024, 256], P('pipe', 'seq')
- filter_grad: float32 [4, 1024, 256], P('pipe', 'seq')
All inputs are finite; a program needn't handle non-finite values.
Results may differ from a plain program's by a relative error of at most 0.001.
Values may be sent and summed in bfloat16 or wider, within the bound.
A program may use at most 64 MiB of HBM per device.

v0:
```python
import math

import jax
import jax.numpy as jnp
from jax import lax
from jax.sharding import PartitionSpec as P

HIGHEST = lax.Precision.HIGHEST


def passed_along(block, axis, distance):
    devices = range(lax.axis_size(axis))
    route = [(i - distance, i) for i in devices if i - distance in devices]
    return lax.ppermute(block, axis, route)


def angle_table(left, right, modulus):
    product = left * right % modulus
    angle = product.astype(jnp.float32) * (2.0 * math.pi / modulus)
    return (jnp.cos(angle), jnp.sin(angle))


def forward_spectrum(signals):
    parts = lax.axis_size("seq")
    rows = signals.shape[1]
    block = rows // parts
    total = 2 * parts * rows
    place = lax.axis_index("seq")
    gathered = lax.all_to_all(signals[:, None], "seq", split_axis=2, concat_axis=1, tiled=True)
    freq_ids = lax.broadcasted_iota(jnp.int32, (2 * parts, parts), 0)
    class_ids = lax.broadcasted_iota(jnp.int32, (2 * parts, parts), 1)
    cos_tab, sin_tab = angle_table(freq_ids, class_ids, 2 * parts)
    real = jnp.einsum("rq,kqjc->krjc", cos_tab, gathered, precision=HIGHEST)
    imag = -jnp.einsum("rq,kqjc->krjc", sin_tab, gathered, precision=HIGHEST)
    freq_grid = lax.broadcasted_iota(jnp.int32, (1, 2 * parts, block, 1), 1)
    row_grid = place * block + lax.broadcasted_iota(jnp.int32, (1, 2 * parts, block, 1), 2)
    tw_cos, tw_sin = angle_table(freq_grid, row_grid, total)
    segment_real = real * tw_cos + imag * tw_sin
    segment_imag = imag * tw_cos - real * tw_sin
    real = lax.all_to_all(segment_real, "seq", split_axis=1, concat_axis=2, tiled=True)
    imag = lax.all_to_all(segment_imag, "seq", split_axis=1, concat_axis=2, tiled=True)
    out_ids = lax.broadcasted_iota(jnp.int32, (rows, rows), 0)
    row_ids = lax.broadcasted_iota(jnp.int32, (rows, rows), 1)
    cos_tab, sin_tab = angle_table(out_ids, row_ids, rows)
    out_real = jnp.einsum("sj,kmjc->kmsc", cos_tab, real, precision=HIGHEST) + jnp.einsum(
        "sj,kmjc->kmsc", sin_tab, imag, precision=HIGHEST
    )
    out_imag = jnp.einsum("sj,kmjc->kmsc", cos_tab, imag, precision=HIGHEST) - jnp.einsum(
        "sj,kmjc->kmsc", sin_tab, real, precision=HIGHEST
    )
    return (out_real, out_imag)


def inverse_signal(real, imag):
    parts = lax.axis_size("seq")
    rows = real.shape[2]
    total = 2 * parts * rows
    place = lax.axis_index("seq")
    row_ids = lax.broadcasted_iota(jnp.int32, (rows, rows), 0)
    out_ids = lax.broadcasted_iota(jnp.int32, (rows, rows), 1)
    cos_tab, sin_tab = angle_table(row_ids, out_ids, rows)
    part_real = jnp.einsum("js,kmsc->kmjc", cos_tab, real, precision=HIGHEST) - jnp.einsum(
        "js,kmsc->kmjc", sin_tab, imag, precision=HIGHEST
    )
    part_imag = jnp.einsum("js,kmsc->kmjc", sin_tab, real, precision=HIGHEST) + jnp.einsum(
        "js,kmsc->kmjc", cos_tab, imag, precision=HIGHEST
    )
    freq_grid = 2 * place + lax.broadcasted_iota(jnp.int32, (1, 2, rows, 1), 1)
    row_grid = lax.broadcasted_iota(jnp.int32, (1, 2, rows, 1), 2)
    tw_cos, tw_sin = angle_table(freq_grid, row_grid, total)
    turned_real = part_real * tw_cos - part_imag * tw_sin
    turned_imag = part_real * tw_sin + part_imag * tw_cos
    gath_real = lax.all_to_all(turned_real, "seq", split_axis=2, concat_axis=1, tiled=True)
    gath_imag = lax.all_to_all(turned_imag, "seq", split_axis=2, concat_axis=1, tiled=True)
    class_ids = lax.broadcasted_iota(jnp.int32, (parts, 2 * parts), 0)
    freq_ids = lax.broadcasted_iota(jnp.int32, (parts, 2 * parts), 1)
    cos_q, sin_q = angle_table(class_ids, freq_ids, 2 * parts)
    factor = 1.0 / total
    value_real = (
        jnp.einsum("qr,krjc->kqjc", cos_q, gath_real, precision=HIGHEST)
        - jnp.einsum("qr,krjc->kqjc", sin_q, gath_imag, precision=HIGHEST)
    ) * factor
    return lax.all_to_all(value_real, "seq", split_axis=1, concat_axis=2, tiled=True)


def per_device(layer_input, filters, skip, incoming, loss_grad):
    received = passed_along(incoming, "pipe", -1)
    is_last = lax.axis_index("pipe") == lax.axis_size("pipe") - 1
    grad_out = jnp.where(is_last, loss_grad[None], received)
    rows = layer_input.shape[1]
    seq_total = rows * lax.axis_size("seq")
    inputs = layer_input[0].astype(jnp.float32)
    grad_vals = grad_out[0].astype(jnp.float32)
    spec_real, spec_imag = forward_spectrum(jnp.stack([inputs, filters[0], grad_vals]))
    in_real, filt_real, grad_real = (spec_real[0], spec_real[1], spec_real[2])
    in_imag, filt_imag, grad_imag = (spec_imag[0], spec_imag[1], spec_imag[2])
    scale = 1.0 / math.sqrt(seq_total)
    adj_real = filt_real * grad_real + filt_imag * grad_imag
    adj_imag = filt_real * grad_imag - filt_imag * grad_real
    corr_real = (grad_real * in_real + grad_imag * in_imag) * scale
    corr_imag = (grad_imag * in_real - grad_real * in_imag) * scale
    results = inverse_signal(jnp.stack([adj_real, corr_real]), jnp.stack([adj_imag, corr_imag]))
    conv_grad = results[0, 0]
    filt_grad = results[1, 0]
    input_grad = (conv_grad + skip[0][None, :] * grad_vals).astype(jnp.bfloat16)
    return (input_grad[None], filt_grad[None])


def solution(mesh):
    return jax.shard_map(
        per_device,
        mesh=mesh,
        in_specs=(
            P("pipe", "seq", None),
            P("pipe", "seq", None),
            P("pipe", None),
            P("pipe", "seq", None),
            P("seq", None),
        ),
        out_specs=(P("pipe", "seq", None), P("pipe", "seq", None)),
        check_vma=False,
    )
```

profile of v0, /device:TPU:0, one launch (start us, length us, event | category | flops | bytes accessed | tf_op | source)
XLA Modules:
  0.0 138.7 jit_solution(7636550546053439250)
XLA Ops:
  0.6 1.3 collective-permute-start
  1.9 0.9 convert_element_type.63
  2.8 1.1 collective-permute-done
  4.1 1.1 copy.67
  5.2 7.3 %all-to-all-start = ((f32[3,1,128,256]{3,1,0,2:T(1,128)}), f32[3,1,128,256]{3,1,0,2:T(1,128)S(1)}, u32[]{:S(2)}, u32[]{:S(2)}) async-start(f32[3,1,128,256]{3,1,0,2:T(1,128)} %copy.67), calls=%async_computation | async-start | bytes 786432 | tf_op jit(solution)/shard_map/all_to_all | solution.py:29
  12.6 11.9 %all-to-all-done = f32[3,1,128,256]{3,1,0,2:T(1,128)S(1)} async-done(((f32[3,1,128,256]{3,1,0,2:T(1,128)}), f32[3,1,128,256]{3,1,0,2:T(1,128)S(1)}, u32[]{:S(2)}, u32[]{:S(2)}) %all-to-all-start) | async-done | bytes 393248 | tf_op jit(solution)/shard_map/all_to_all | solution.py:29
  24.5 1.0 convolution_bitcast_fusion
  25.5 1.2 multiply_add_fusion
  26.7 1.4 copy.71
  28.1 4.6 %all-to-all-start.1 = ((f32[3,16,16,256]{3,2,0,1:T(8,128)}), f32[3,16,16,256]{3,2,0,1:T(8,128)S(1)}, u32[]{:S(2)}, u32[]{:S(2)}) async-start(f32[3,16,16,256]{3,2,0,1:T(8,128)} %copy.71), calls=%async_computation.1 | async-start | bytes 1572864 | tf_op jit(solution)/shard_map/all_to_all | solution.py:40
  32.7 1.3 copy.75
  34.0 19.1 %all-to-all-done.1 = f32[3,16,16,256]{3,2,0,1:T(8,128)S(1)} async-done(((f32[3,16,16,256]{3,2,0,1:T(8,128)}), f32[3,16,16,256]{3,2,0,1:T(8,128)S(1)}, u32[]{:S(2)}, u32[]{:S(2)}) %all-to-all-start.1) | async-done | bytes 786464 | tf_op jit(solution)/shard_map/all_to_all | solution.py:40
  53.1 3.7 %all-to-all-start.2 = ((f32[3,16,16,256]{3,2,0,1:T(8,128)}), f32[3,16,16,256]{3,2,0,1:T(8,128)S(1)}, u32[]{:S(2)}, u32[]{:S(2)}) async-start(f32[3,16,16,256]{3,2,0,1:T(8,128)} %copy.75), calls=%async_computation.2 | async-start | bytes 1572864 | tf_op jit(solution)/shard_map/all_to_all | solution.py:41
  57.1 1.5 %fusion.20 = f32[3,2,256,128]{3,2,1,0:T(8,128)S(1)} fusion(f32[3,2,128,256]{3,2,1,0:T(8,128)S(1)} %bitcast.98), kind=kOutput, calls=%fused_computation.42 | convolution fusion | flops 302219264 | bytes 1572864 | tf_op jit(solution)/shard_map/sj,kmjc->kmsc/dot_general | solution.py:45
  58.6 18.5 %all-to-all-done.2 = f32[3,16,16,256]{3,2,0,1:T(8,128)S(1)} async-done(((f32[3,16,16,256]{3,2,0,1:T(8,128)}), f32[3,16,16,256]{3,2,0,1:T(8,128)S(1)}, u32[]{:S(2)}, u32[]{:S(2)}) %all-to-all-start.2) | async-done | bytes 786464 | tf_op jit(solution)/shard_map/all_to_all | solution.py:41
  77.2 1.5 %fusion.18 = f32[3,2,256,128]{3,2,1,0:T(8,128)S(1)} fusion(f32[3,2,128,256]{3,2,1,0:T(8,128)S(1)} %bitcast.100), kind=kOutput, calls=%fused_computation.40 | convolution fusion | flops 302219264 | bytes 1572864 | tf_op jit(solution)/shard_map/sj,kmjc->kmsc/dot_general | solution.py:48
  78.7 1.5 %fusion.1 = f32[3,2,128,256]{2,3,1,0:T(8,128)S(1)} fusion(f32[3,2,256,128]{3,2,1,0:T(8,128)S(1)} %fusion.20, f32[3,2,128,256]{3,2,1,0:T(8,128)S(1)} %bitcast.101), kind=kOutput, calls=%fused_computation.3 | convolution fusion | flops 302415872 | bytes 2359296 | tf_op jit(solution)/shard_map/sj,kmjc->kmsc/dot_general | solution.py:45
  80.2 1.5 %fusion = f32[3,2,128,256]{2,3,1,0:T(8,128)S(1)} fusion(f32[3,2,256,128]{3,2,1,0:T(8,128)S(1)} %fusion.18, f32[3,2,128,256]{3,2,1,0:T(8,128)S(1)} %bitcast.99), kind=kOutput, calls=%fused_computation.1 | convolution fusion | flops 302415872 | bytes 2359296 | tf_op jit(solution)/shard_map/sj,kmjc->kmsc/dot_general | solution.py:48
  81.9 0.8 fusion.6
  82.7 0.8 fusion.5
  83.5 0.8 convolution_add_fusion.1
  84.4 0.9 add_bitcast_fusion
  85.2 1.0 copy.81
  86.3 3.5 %all-to-all-start.3 = ((f32[2,2,128,256]{3,1,0,2:T(2,128)}), f32[2,2,128,256]{3,1,0,2:T(2,128)S(1)}, u32[]{:S(2)}, u32[]{:S(2)}) async-start(f32[2,2,128,256]{3,1,0,2:T(2,128)} %copy.81), calls=%async_computation.3 | async-start | bytes 1048576 | tf_op jit(solution)/shard_map/all_to_all | solution.py:73
  89.8 1.0 copy.84
  90.8 13.7 %all-to-all-done.3 = f32[2,2,128,256]{3,1,0,2:T(2,128)S(1)} async-done(((f32[2,2,128,256]{3,1,0,2:T(2,128)}), f32[2,2,128,256]{3,1,0,2:T(2,128)S(1)}, u32[]{:S(2)}, u32[]{:S(2)}) %all-to-all-start.3) | async-done | bytes 524320 | tf_op jit(solution)/shard_map/all_to_all | solution.py:73
  104.5 3.7 %all-to-all-start.4 = ((f32[2,2,128,256]{3,1,0,2:T(2,128)}), f32[2,2,128,256]{3,1,0,2:T(2,128)S(1)}, u32[]{:S(2)}, u32[]{:S(2)}) async-start(f32[2,2,128,256]{3,1,0,2:T(2,128)} %copy.84), calls=%async_computation.4 | async-start | bytes 1048576 | tf_op jit(solution)/shard_map/all_to_all | solution.py:74
  109.5 13.3 %all-to-all-done.4 = f32[2,2,128,256]{3,1,0,2:T(2,128)S(1)} async-done(((f32[2,2,128,256]{3,1,0,2:T(2,128)}), f32[2,2,128,256]{3,1,0,2:T(2,128)S(1)}, u32[]{:S(2)}, u32[]{:S(2)}) %all-to-all-start.4) | async-done | bytes 524320 | tf_op jit(solution)/shard_map/all_to_all | solution.py:74
  124.2 12.5 %all_to_all.93 = f32[2,8,16,256]{3,2,0,1:T(8,128)S(1)} all-to-all(f32[2,8,16,256]{3,2,0,1:T(8,128)S(1)} %copy.87), channel_id=1, replica_groups=mesh['pipe'=4,'seq'=8] {'seq'}, dimensions={1} | all-to-all | bytes 524288 | tf_op jit(solution)/shard_map/all_to_all | solution.py:83
  136.7 0.7 fusion.126
  137.4 0.7 copy-done.2
  138.1 0.6 add_convert_fusion
  (24 shorter events, 3.3 us)
Async XLA Ops:
  0.6 3.4 %collective-permute-start = (bf16[1,128,256]{2,1,0:T(8,128)(2,1)}, bf16[1,128,256]{2,1,0:T(8,128)(2,1)S(1)}, u32[]{:S(2)}, u32[]{:S(2)}) collective-permute-start(bf16[1,128,256]{2,1,0:T(8,128)(2,1)} %param.8), channel_id=1, source_target_pairs={{8,0},{16,8},{24,16},{9,1},{17,9},{25,17},{10,2},{18,10},{26,18},{... | collective-permute-start | bytes 196616 | tf_op jit(solution)/shard_map/ppermute | solution.py:14
  1.9 2.1 %copy-start.1 = (bf16[128,256]{1,0:T(8,128)(2,1)S(1)}, bf16[128,256]{1,0:T(8,128)(2,1)}, u32[]{:S(2)}) copy-start(bf16[128,256]{1,0:T(8,128)(2,1)} %param.9) | copy-start | bytes 196612
  2.8 1.2 copy-start
  5.2 19.3 %all-to-all-start = ((f32[3,1,128,256]{3,1,0,2:T(1,128)}), f32[3,1,128,256]{3,1,0,2:T(1,128)S(1)}, u32[]{:S(2)}, u32[]{:S(2)}) async-start(f32[3,1,128,256]{3,1,0,2:T(1,128)} %copy.67), calls=%async_computation | async-start | bytes 786432 | tf_op jit(solution)/shard_map/all_to_all | solution.py:29
  28.1 25.0 %all-to-all-start.1 = ((f32[3,16,16,256]{3,2,0,1:T(8,128)}), f32[3,16,16,256]{3,2,0,1:T(8,128)S(1)}, u32[]{:S(2)}, u32[]{:S(2)}) async-start(f32[3,16,16,256]{3,2,0,1:T(8,128)} %copy.71), calls=%async_computation.1 | async-start | bytes 1572864 | tf_op jit(solution)/shard_map/all_to_all | solution.py:40
  53.1 24.0 %all-to-all-start.2 = ((f32[3,16,16,256]{3,2,0,1:T(8,128)}), f32[3,16,16,256]{3,2,0,1:T(8,128)S(1)}, u32[]{:S(2)}, u32[]{:S(2)}) async-start(f32[3,16,16,256]{3,2,0,1:T(8,128)} %copy.75), calls=%async_computation.2 | async-start | bytes 1572864 | tf_op jit(solution)/shard_map/all_to_all | solution.py:41
  86.3 18.2 %all-to-all-start.3 = ((f32[2,2,128,256]{3,1,0,2:T(2,128)}), f32[2,2,128,256]{3,1,0,2:T(2,128)S(1)}, u32[]{:S(2)}, u32[]{:S(2)}) async-start(f32[2,2,128,256]{3,1,0,2:T(2,128)} %copy.81), calls=%async_computation.3 | async-start | bytes 1048576 | tf_op jit(solution)/shard_map/all_to_all | solution.py:73
  104.5 18.3 %all-to-all-start.4 = ((f32[2,2,128,256]{3,1,0,2:T(2,128)}), f32[2,2,128,256]{3,1,0,2:T(2,128)S(1)}, u32[]{:S(2)}, u32[]{:S(2)}) async-start(f32[2,2,128,256]{3,1,0,2:T(2,128)} %copy.84), calls=%async_computation.4 | async-start | bytes 1048576 | tf_op jit(solution)/shard_map/all_to_all | solution.py:74
  137.4 0.7 copy-start.2
where the time goes:
time: 139 us
  waiting for transfers between devices  77.5 us (56%)
  starting transfers between devices  24.2 us (17%)
  blocking collectives  12.5 us (9%)
  matrix products  12.4 us (9%)
  local copies, waits for them, and re-layouts  9.2 us (7%)
  other arithmetic  1.96 us (1%)
    all_to_all x1, waiting for transfers between devices, forward_spectrum(): lax.all_to_all(segment_real, 'seq', split_axis=1, concat_axis=2, tiled=True)  19.1 us
    all_to_all x1, waiting for transfers between devices, forward_spectrum(): lax.all_to_all(segment_imag, 'seq', split_axis=1, concat_axis=2, tiled=True)  18.5 us
    all_to_all x1, waiting for transfers between devices, inverse_signal(): lax.all_to_all(turned_real, 'seq', split_axis=2, concat_axis=1, tiled=True)  13.7 us
    all_to_all x1, waiting for transfers between devices, inverse_signal(): lax.all_to_all(turned_imag, 'seq', split_axis=2, concat_axis=1, tiled=True)  13.3 us
    all_to_all x1, blocking collectives, inverse_signal(): lax.all_to_all(value_real, 'seq', split_axis=1, concat_axis=2, tiled=True)  12.5 us
    all_to_all x1, waiting for transfers between devices, forward_spectrum(): lax.all_to_all(signals[:, None], 'seq', split_axis=2, concat_axis=1, tile...  11.9 us
    all_to_all x1, starting transfers between devices, forward_spectrum(): lax.all_to_all(signals[:, None], 'seq', split_axis=2, concat_axis=1, tile...  7.28 us
    all_to_all x1, starting transfers between devices, forward_spectrum(): lax.all_to_all(segment_real, 'seq', split_axis=1, concat_axis=2, tiled=True)  4.61 us
  transfers between devices with their start and end apart: 6, of which 6 were waited for; matrix products, arithmetic and copies ran while one was open for 4% of the time, Pallas kernels for 0%

commit v1 on v0

--- a/solution.py
+++ b/solution.py
@@ -1,10 +1,14 @@
+import functools
 import math
 
 import jax
 import jax.numpy as jnp
 from jax import lax
+from jax.experimental import pallas as pl
+from jax.experimental.pallas import tpu as pltpu
 from jax.sharding import PartitionSpec as P
 
+MESH = pl.DeviceIdType.MESH
 HIGHEST = lax.Precision.HIGHEST
 
 
@@ -106,9 +110,175 @@
     return (input_grad[None], filt_grad[None])
 
 
+def remote(src, dst, send_sem, recv_sem, device):
+    return pltpu.make_async_remote_copy(
+        src_ref=src, dst_ref=dst, send_sem=send_sem, recv_sem=recv_sem, device_id=device, device_id_type=MESH
+    )
+
+
+def correlate_kernel(
+    pipes, parts, x_ref, f_ref, skip_ref, inc_ref, loss_ref, ig_ref, fg_ref,
+    x_out, f_out, g_out, x_in, g_in, f_pad, x_pad, g_val, conv, corr, conv_out, ig_in, fg_in,
+    x_send, x_recv, f_send, f_recv, g_send, g_recv, ig_send, ig_recv, fg_send, fg_recv,
+):
+    section = lax.axis_index("pipe")
+    me = lax.axis_index("seq")
+    rows = x_ref.shape[0]
+    chans = x_ref.shape[1] // parts
+    before = lax.rem(section + pipes - 1, pipes)
+    after = lax.rem(section + 1, pipes)
+    others = [lax.rem(me + k, parts) for k in range(parts)]
+
+    def part(ref, index, size=chans, start=0):
+        return ref.at[pl.ds(pl.multiple_of(index * chans + start, 16), size)]
+
+    barrier = pltpu.get_barrier_semaphore()
+    for k in range(parts):
+        if k:
+            pl.semaphore_signal(barrier, inc=1, device_id=(section, others[k]), device_id_type=MESH)
+        pl.semaphore_signal(barrier, inc=1, device_id=(after, others[k]), device_id_type=MESH)
+
+    grad = jnp.where(section == 0, loss_ref[...].astype(jnp.float32), inc_ref[...].astype(jnp.float32))
+    g_out[...] = grad.T.astype(jnp.bfloat16)
+    row_ids = lax.broadcasted_iota(jnp.int32, (rows, rows), 0)
+    col_ids = lax.broadcasted_iota(jnp.int32, (rows, rows), 1)
+    flip = jnp.where(row_ids + col_ids == rows - 1, 1.0, 0.0).astype(jnp.bfloat16)
+    x_out[...] = jnp.dot(flip, x_ref[...], preferred_element_type=jnp.float32).T.astype(jnp.bfloat16)
+    filt = f_ref[...]
+    filt_hi = filt.astype(jnp.bfloat16)
+    filt_lo = (filt - filt_hi.astype(jnp.float32)).astype(jnp.bfloat16)
+    f_out[...] = (
+        jnp.dot(flip, filt_hi, preferred_element_type=jnp.float32)
+        + jnp.dot(flip, filt_lo, preferred_element_type=jnp.float32)
+    ).T
+    half = parts * chans
+    f_pad[half:, :] = jnp.zeros((half, rows), jnp.float32)
+    x_pad[half:, :] = jnp.zeros((half, rows), jnp.float32)
+
+    pl.semaphore_wait(barrier, 2 * parts - 1)
+
+    sends = []
+    for k in range(parts):
+        to = others[k]
+        sends.append(remote(part(g_out, to), part(g_in, me), g_send.at[k], g_recv.at[k], (before, to)))
+        sends[-1].start()
+    for k in range(1, parts):
+        to = others[k]
+        sends.append(remote(part(x_out, to), part(x_in, parts - 1 - me), x_send.at[k], x_recv.at[k], (section, to)))
+        sends[-1].start()
+        sends.append(remote(part(f_out, to), part(f_pad, parts - 1 - me), f_send.at[k], f_recv.at[k], (section, to)))
+        sends[-1].start()
+    part(f_pad, parts - 1 - me)[...] = part(f_out, me)[...]
+    part(x_in, parts - 1 - me)[...] = part(x_out, me)[...]
+    for copy in sends:
+        copy.wait_recv()
+    g_val[...] = g_in[...].astype(jnp.float32)
+    x_pad[:half, :] = x_in[...].astype(jnp.float32)
+
+    keep = col_ids <= row_ids
+
+    def streams(ref, chan):
+        pieces = [ref[pl.ds((parts - 1 - e) * chans + chan, parts, stride=chans), :] for e in range(parts)]
+        return jnp.concatenate(pieces, axis=1)
+
+    def hankel(chan):
+        turned = []
+        for e in range(parts):
+            row = jnp.broadcast_to(g_val[pl.ds(e * chans + chan, 1), :], (rows, rows))
+            turned.append(pltpu.roll(row, 1, 1, stride=1, stride_axis=0))
+        turned.append(jnp.zeros((rows, rows), jnp.float32))
+        return jnp.concatenate(
+            [jnp.where(keep, turned[e], turned[e + 1]).astype(jnp.bfloat16) for e in range(parts)], axis=0
+        )
+
+    def pair(first):
+        left, right = [], []
+        for chan in (first, first + 1):
+            filt = streams(f_pad, chan)
+            hi = filt.astype(jnp.bfloat16).astype(jnp.float32)
+            left += [hi, filt - hi, streams(x_pad, chan)]
+            right.append(hankel(chan))
+        result = jnp.dot(
+            jnp.concatenate(left, axis=0).astype(jnp.bfloat16),
+            jnp.concatenate(right, axis=1),
+            preferred_element_type=jnp.float32,
+        )
+        for i in range(2):
+            chan = first + i
+            mine = result[3 * parts * i : 3 * parts * (i + 1), rows * i : rows * (i + 1)]
+            where = pl.ds(chan, parts, stride=chans)
+            gain = skip_ref[0, me * chans + chan]
+            conv[where, :] = mine[:parts] + mine[parts : 2 * parts] + gain * g_val[where, :]
+            corr[where, :] = mine[2 * parts :] * (1.0 / math.sqrt(rows * parts))
+
+    returns = []
+    size = chans // 2
+    for h in range(2):
+        def body(i, carry):
+            pair(h * size + 2 * i)
+            return carry
+
+        lax.fori_loop(0, size // 2, body, 0)
+        for a in range(parts):
+            span = pl.ds(a * chans + h * size, size)
+            conv_out[span, :] = conv[span, :].astype(jnp.bfloat16)
+        for k in range(1, parts):
+            to = others[k]
+            sems = (ig_send.at[h, k], ig_recv.at[h, k])
+            returns.append(
+                remote(part(conv_out, to, size, h * size), part(ig_in, me, size, h * size), *sems, (section, to))
+            )
+            returns[-1].start()
+            sems = (fg_send.at[h, k], fg_recv.at[h, k])
+            returns.append(
+                remote(part(corr, to, size, h * size), part(fg_in, me, size, h * size), *sems, (section, to))
+            )
+            returns[-1].start()
+    part(ig_in, me)[...] = part(conv_out, me)[...]
+    part(fg_in, me)[...] = part(corr, me)[...]
+    for copy in returns:
+        copy.wait_recv()
+    ig_ref[...] = ig_in[...].astype(jnp.float32).T.astype(jnp.bfloat16)
+    fg_ref[...] = fg_in[...].T
+    for copy in sends + returns:
+        copy.wait_send()
+
+
+def kernel_per_device(pipes, parts, layer_input, filters, skip, incoming, loss_grad):
+    rows, width = loss_grad.shape
+    vmem = pl.BlockSpec(memory_space=pltpu.VMEM)
+    narrow = pltpu.VMEM((width, rows), jnp.bfloat16)
+    wide = pltpu.VMEM((width, rows), jnp.float32)
+    padded = pltpu.VMEM((2 * width, rows), jnp.float32)
+    sems = [pltpu.SemaphoreType.DMA((parts,))] * 6 + [pltpu.SemaphoreType.DMA((2, parts))] * 4
+    input_grad, filter_grad = pl.pallas_call(
+        functools.partial(correlate_kernel, pipes, parts),
+        out_shape=(
+            jax.ShapeDtypeStruct((rows, width), jnp.bfloat16),
+            jax.ShapeDtypeStruct((rows, width), jnp.float32),
+        ),
+        in_specs=[vmem, vmem, pl.BlockSpec(memory_space=pltpu.SMEM), vmem, vmem],
+        out_specs=(vmem, vmem),
+        scratch_shapes=[narrow, wide, narrow, narrow, narrow, padded, padded, wide, wide, wide, narrow, narrow, wide]
+        + sems,
+        compiler_params=pltpu.CompilerParams(
+            collective_id=0, has_side_effects=True, vmem_limit_bytes=32 * 1024 * 1024
+        ),
+    )(layer_input[0], filters[0], skip, incoming[0], loss_grad)
+    return (input_grad[None], filter_grad[None])
+
+
 def solution(mesh):
+    pipes, parts = mesh.shape["pipe"], mesh.shape["seq"]
+
+    def step(layer_input, filters, skip, incoming, loss_grad):
+        rows, width = loss_grad.shape
+        if pipes > 1 and parts == 8 and rows == 128 and width % (32 * parts) == 0:
+            return kernel_per_device(pipes, parts, layer_input, filters, skip, incoming, loss_grad)
+        return per_device(layer_input, filters, skip, incoming, loss_grad)
+
     return jax.shard_map(
-        per_device,
+        step,
         mesh=mesh,
         in_specs=(
             P("pipe", "seq", None),

time: 139 us -> 33 us (0.24)
  waiting for transfers between devices: 77.5 us -> 0 us
  Pallas kernels: 0 us -> 26.7 us
  starting transfers between devices: 24.2 us -> 0 us
  blocking collectives: 12.5 us -> 0 us
  matrix products: 12.4 us -> 0 us
  local copies, waits for them, and re-layouts: 9.2 us -> 5.38 us
  other arithmetic: 1.96 us -> 0 us
    all_to_all x5 -> x0, waiting for transfers between devices: 76.4 us -> none  [the longest x1 19.1 us: forward_spectrum(): lax.all_to_all(segment_real, 'seq', split_axis=1, concat_axis=2, tiled=True)]
    pallas_call x0 -> x1, Pallas kernels: none -> 26.7 us  [kernel_per_device(): pl.pallas_call(functools.partial(correlate_kernel, pipes, parts), out_sha...]
    all_to_all x5 -> x0, starting transfers between devices: 22.9 us -> none  [the longest x1 7.28 us: forward_spectrum(): lax.all_to_all(signals[:, None], 'seq', split_axis=2, concat_axis=1, tile...]
    all_to_all x1 -> x0, blocking collectives: 12.5 us -> none  [inverse_signal(): lax.all_to_all(value_real, 'seq', split_axis=1, concat_axis=2, tiled=True)]
    dot_general x12 -> x0, matrix products: 12.4 us -> none  [the longest x1 1.52 us: forward_spectrum(): jnp.einsum('sj,kmjc->kmsc', cos_tab, real, precision=HIGHEST)]
    unnamed x6 -> x12, local copies, waits for them, and re-layouts: 0.69 us -> 5.38 us
    add x2 -> x0, local copies, waits for them, and re-layouts: 2.36 us -> none  [the longest x1 1.37 us: forward_spectrum(): segment_real = real * tw_cos + imag * tw_sin]
    sub x2 -> x0, local copies, waits for them, and re-layouts: 2.35 us -> none  [the longest x1 1.35 us: forward_spectrum(): segment_imag = imag * tw_cos - real * tw_sin]
  transfers between devices with their start and end apart: 6 -> 0, of which waited for: 6 -> 0; matrix products, arithmetic and copies ran while one was open for 4% -> 0% of each run, Pallas kernels for 0% -> 0%
where the time goes in v1:
time: 33 us; the launch traced here: 32.7 us
  Pallas kernels  26.7 us (81%)
  local copies, waits for them, and re-layouts  5.38 us (16%)
  between operations  0.65 us (2%)
    pallas_call x1, Pallas kernels, kernel_per_device(): pl.pallas_call(functools.partial(correlate_kernel, pipes, parts), out_sha...  26.7 us
    unnamed x12, local copies, waits for them, and re-layouts  5.38 us

profile of v1, /device:TPU:0, one launch (start us, length us, event | category | flops | bytes accessed | tf_op | source)
XLA Modules:
  0.0 32.7 jit_solution(16560097496882243128)
XLA Ops:
  0.6 0.0 copy-start.4
  0.6 0.7 %copy-done.4 = f32[1,256]{1,0:T(1,128)S(1)} copy-done((f32[1,256]{1,0:T(1,128)S(1)}, f32[1,256]{1,0:T(1,128)}, u32[]{:S(2)}) %copy-start.4) | copy-done | bytes 1048
  1.3 0.0 copy-start
  1.3 0.9 %copy-done = f32[1,128,256]{2,1,0:T(8,128)S(1)} copy-done((f32[1,128,256]{2,1,0:T(8,128)S(1)}, f32[1,128,256]{2,1,0:T(8,128)}, u32[]{:S(2)}) %copy-start) | copy-done | bytes 131096
  2.2 0.0 copy-start.1
  2.2 0.8 %copy-done.1 = bf16[1,128,256]{2,1,0:T(8,128)(2,1)S(1)} copy-done((bf16[1,128,256]{2,1,0:T(8,128)(2,1)S(1)}, bf16[1,128,256]{2,1,0:T(8,128)(2,1)}, u32[]{:S(2)}) %copy-start.1) | copy-done | bytes 65560
  3.1 0.0 copy-start.2
  3.1 0.8 %copy-done.2 = bf16[1,128,256]{2,1,0:T(8,128)(2,1)S(1)} copy-done((bf16[1,128,256]{2,1,0:T(8,128)(2,1)S(1)}, bf16[1,128,256]{2,1,0:T(8,128)(2,1)}, u32[]{:S(2)}) %copy-start.2) | copy-done | bytes 65560
  3.9 0.0 copy-start.3
  3.9 0.8 %copy-done.3 = bf16[128,256]{1,0:T(8,128)(2,1)S(1)} copy-done((bf16[128,256]{1,0:T(8,128)(2,1)S(1)}, bf16[128,256]{1,0:T(8,128)(2,1)}, u32[]{:S(2)}) %copy-start.3) | copy-done | bytes 65560
  4.7 26.7 %shard_map.68 = (bf16[128,256]{1,0:T(8,128)(2,1)S(1)}, f32[128,256]{1,0:T(8,128)S(1)}) custom-call(bf16[128,256]{1,0:T(8,128)(2,1)S(1)} %bitcast.7, f32[128,256]{1,0:T(8,128)S(1)} %bitcast.5, f32[1,256]{1,0:T(1,128)S(1)} %copy-done.4, bf16[128,256]{1,0:T(8,128)(2,1)S(1)} %bitcast.8, bf16[128,256]{1,0:T(8,128)(2,1)S(1)} %copy-done.3), custom_call_target="tpu_custom_call" | custom-call | tf_op jit(solution)/shard_map/pallas_call | solution.py:254
  31.4 0.6 %copy.9 = bf16[1,128,256]{2,1,0:T(8,128)(2,1)} copy(bf16[1,128,256]{2,1,0:T(8,128)(2,1)S(1)} %bitcast.9) | data formatting | bytes 131072
  32.0 0.7 %copy.10 = f32[1,128,256]{2,1,0:T(8,128)} copy(f32[1,128,256]{2,1,0:T(8,128)S(1)} %bitcast.6) | data formatting | bytes 262144
Async XLA Ops:
  0.6 0.7 %copy-start.4 = (f32[1,256]{1,0:T(1,128)S(1)}, f32[1,256]{1,0:T(1,128)}, u32[]{:S(2)}) copy-start(f32[1,256]{1,0:T(1,128)} %skip_ref.1) | copy-start | bytes 3076
  1.3 0.9 %copy-start = (f32[1,128,256]{2,1,0:T(8,128)S(1)}, f32[1,128,256]{2,1,0:T(8,128)}, u32[]{:S(2)}) copy-start(f32[1,128,256]{2,1,0:T(8,128)} %param.6) | copy-start | bytes 393220
  2.2 0.8 %copy-start.1 = (bf16[1,128,256]{2,1,0:T(8,128)(2,1)S(1)}, bf16[1,128,256]{2,1,0:T(8,128)(2,1)}, u32[]{:S(2)}) copy-start(bf16[1,128,256]{2,1,0:T(8,128)(2,1)} %param.5) | copy-start | bytes 196612
  3.1 0.8 %copy-start.2 = (bf16[1,128,256]{2,1,0:T(8,128)(2,1)S(1)}, bf16[1,128,256]{2,1,0:T(8,128)(2,1)}, u32[]{:S(2)}) copy-start(bf16[1,128,256]{2,1,0:T(8,128)(2,1)} %param.8) | copy-start | bytes 196612
  3.9 0.8 %copy-start.3 = (bf16[128,256]{1,0:T(8,128)(2,1)S(1)}, bf16[128,256]{1,0:T(8,128)(2,1)}, u32[]{:S(2)}) copy-start(bf16[128,256]{1,0:T(8,128)(2,1)} %loss_ref.1) | copy-start | bytes 196612

commit v2 on v1

--- a/solution.py
+++ b/solution.py
@@ -110,6 +110,9 @@
     return (input_grad[None], filt_grad[None])
 
 
+SIZE = 16
+
+
 def remote(src, dst, send_sem, recv_sem, device):
     return pltpu.make_async_remote_copy(
         src_ref=src, dst_ref=dst, send_sem=send_sem, recv_sem=recv_sem, device_id=device, device_id_type=MESH
@@ -117,20 +120,33 @@
 
 
 def correlate_kernel(
-    pipes, parts, x_ref, f_ref, skip_ref, inc_ref, loss_ref, ig_ref, fg_ref,
-    x_out, f_out, g_out, x_in, g_in, f_pad, x_pad, g_val, conv, corr, conv_out, ig_in, fg_in,
-    x_send, x_recv, f_send, f_recv, g_send, g_recv, ig_send, ig_recv, fg_send, fg_recv,
+    pipes, parts, x_hbm, f_hbm, skip_hbm, inc_hbm, loss_hbm, ig_ref, fg_ref,
+    x_ref, f_ref, grad_ref, skip_ref, s_out, s_in, g_out, g_in, pads, g_val, conv, corr, r_out, r_in,
+    load_sem, s_send, s_recv, g_send, g_recv, r_send, r_recv,
 ):
     section = lax.axis_index("pipe")
     me = lax.axis_index("seq")
     rows = x_ref.shape[0]
     chans = x_ref.shape[1] // parts
+    chunks = chans // SIZE
     before = lax.rem(section + pipes - 1, pipes)
     after = lax.rem(section + 1, pipes)
     others = [lax.rem(me + k, parts) for k in range(parts)]
 
-    def part(ref, index, size=chans, start=0):
-        return ref.at[pl.ds(pl.multiple_of(index * chans + start, 16), size)]
+    @pl.when(section == 0)
+    def _():
+        pltpu.make_async_copy(loss_hbm, grad_ref, load_sem.at[0]).start()
+
+    @pl.when(section != 0)
+    def _():
+        pltpu.make_async_copy(inc_hbm, grad_ref, load_sem.at[0]).start()
+
+    load_f = pltpu.make_async_copy(f_hbm, f_ref, load_sem.at[1])
+    load_x = pltpu.make_async_copy(x_hbm, x_ref, load_sem.at[2])
+    load_skip = pltpu.make_async_copy(skip_hbm, skip_ref, load_sem.at[3])
+    load_f.start()
+    load_x.start()
+    load_skip.start()
 
     barrier = pltpu.get_barrier_semaphore()
     for k in range(parts):
@@ -138,47 +154,59 @@
             pl.semaphore_signal(barrier, inc=1, device_id=(section, others[k]), device_id_type=MESH)
         pl.semaphore_signal(barrier, inc=1, device_id=(after, others[k]), device_id_type=MESH)
 
-    grad = jnp.where(section == 0, loss_ref[...].astype(jnp.float32), inc_ref[...].astype(jnp.float32))
-    g_out[...] = grad.T.astype(jnp.bfloat16)
     row_ids = lax.broadcasted_iota(jnp.int32, (rows, rows), 0)
     col_ids = lax.broadcasted_iota(jnp.int32, (rows, rows), 1)
     flip = jnp.where(row_ids + col_ids == rows - 1, 1.0, 0.0).astype(jnp.bfloat16)
-    x_out[...] = jnp.dot(flip, x_ref[...], preferred_element_type=jnp.float32).T.astype(jnp.bfloat16)
+    for kind in range(3):
+        pads[kind, parts * chans :, :] = jnp.zeros((parts * chans, rows), jnp.float32)
+
+    def turned_over(block):
+        return jnp.dot(flip, block, preferred_element_type=jnp.float32).T.astype(jnp.bfloat16)
+
+    def place(kind, block):
+        for c in range(parts):
+            for h in range(chunks):
+                start = c * chans + h * SIZE
+                s_out[c, h, kind * SIZE : (kind + 1) * SIZE, :] = block[start : start + SIZE]
+
+    pltpu.make_async_copy(inc_hbm, grad_ref, load_sem.at[0]).wait()
+    g_out[...] = grad_ref[...].astype(jnp.float32).T.astype(jnp.bfloat16)
+    load_f.wait()
     filt = f_ref[...]
     filt_hi = filt.astype(jnp.bfloat16)
-    filt_lo = (filt - filt_hi.astype(jnp.float32)).astype(jnp.bfloat16)
-    f_out[...] = (
-        jnp.dot(flip, filt_hi, preferred_element_type=jnp.float32)
-        + jnp.dot(flip, filt_lo, preferred_element_type=jnp.float32)
-    ).T
-    half = parts * chans
-    f_pad[half:, :] = jnp.zeros((half, rows), jnp.float32)
-    x_pad[half:, :] = jnp.zeros((half, rows), jnp.float32)
+    place(0, turned_over(filt_hi))
+    place(1, turned_over((filt - filt_hi.astype(jnp.float32)).astype(jnp.bfloat16)))
+    load_x.wait()
+    place(2, turned_over(x_ref[...]))
 
     pl.semaphore_wait(barrier, 2 * parts - 1)
 
+    def span(index, h):
+        return pl.ds(pl.multiple_of(index * chans + h * SIZE, SIZE), SIZE)
+
+    slot = parts - 1 - me
     sends = []
-    for k in range(parts):
-        to = others[k]
-        sends.append(remote(part(g_out, to), part(g_in, me), g_send.at[k], g_recv.at[k], (before, to)))
-        sends[-1].start()
-    for k in range(1, parts):
-        to = others[k]
-        sends.append(remote(part(x_out, to), part(x_in, parts - 1 - me), x_send.at[k], x_recv.at[k], (section, to)))
-        sends[-1].start()
-        sends.append(remote(part(f_out, to), part(f_pad, parts - 1 - me), f_send.at[k], f_recv.at[k], (section, to)))
-        sends[-1].start()
-    part(f_pad, parts - 1 - me)[...] = part(f_out, me)[...]
-    part(x_in, parts - 1 - me)[...] = part(x_out, me)[...]
-    for copy in sends:
-        copy.wait_recv()
-    g_val[...] = g_in[...].astype(jnp.float32)
-    x_pad[:half, :] = x_in[...].astype(jnp.float32)
+    for h in range(chunks):
+        group = []
+        for k in range(parts):
+            to = others[k]
+            sems = (g_send.at[h, k], g_recv.at[h, k])
+            group.append(remote(g_out.at[span(to, h)], g_in.at[span(me, h)], *sems, (before, to)))
+            group[-1].start()
+            if k:
+                sems = (s_send.at[h, k], s_recv.at[h, k])
+                group.append(remote(s_out.at[to, h], s_in.at[slot, h], *sems, (section, to)))
+                group[-1].start()
+        sends.append(group)
+    s_in[slot] = s_out[me]
+    load_skip.wait()
 
     keep = col_ids <= row_ids
 
-    def streams(ref, chan):
-        pieces = [ref[pl.ds((parts - 1 - e) * chans + chan, parts, stride=chans), :] for e in range(parts)]
+    def streams(kind, chan):
+        pieces = [
+            pads[kind, pl.ds((parts - 1 - e) * chans + chan, parts, stride=chans), :] for e in range(parts)
+        ]
         return jnp.concatenate(pieces, axis=1)
 
     def hankel(chan):
@@ -194,9 +222,7 @@
     def pair(first):
         left, right = [], []
         for chan in (first, first + 1):
-            filt = streams(f_pad, chan)
-            hi = filt.astype(jnp.bfloat16).astype(jnp.float32)
-            left += [hi, filt - hi, streams(x_pad, chan)]
+            left += [streams(kind, chan) for kind in range(3)]
             right.append(hankel(chan))
         result = jnp.dot(
             jnp.concatenate(left, axis=0).astype(jnp.bfloat16),
@@ -212,57 +238,86 @@
             corr[where, :] = mine[2 * parts :] * (1.0 / math.sqrt(rows * parts))
 
     returns = []
-    size = chans // 2
-    for h in range(2):
+    for h in range(chunks):
+        for copy in sends[h]:
+            copy.wait_recv()
+        for e in range(parts):
+            held = slice(e * chans + h * SIZE, e * chans + (h + 1) * SIZE)
+            g_val[held, :] = g_in[held, :].astype(jnp.float32)
+            for kind in range(3):
+                pads[kind, held, :] = s_in[e, h, kind * SIZE : (kind + 1) * SIZE, :].astype(jnp.float32)
+
         def body(i, carry):
-            pair(h * size + 2 * i)
+            pair(h * SIZE + 2 * i)
             return carry
 
-        lax.fori_loop(0, size // 2, body, 0)
+        lax.fori_loop(0, SIZE // 2, body, 0, unroll=2)
         for a in range(parts):
-            span = pl.ds(a * chans + h * size, size)
-            conv_out[span, :] = conv[span, :].astype(jnp.bfloat16)
+            held = slice(a * chans + h * SIZE, a * chans + (h + 1) * SIZE)
+            value = corr[held, :]
+            value_hi = value.astype(jnp.bfloat16)
+            r_out[a, h, :SIZE, :] = conv[held, :].astype(jnp.bfloat16)
+            r_out[a, h, SIZE : 2 * SIZE, :] = value_hi
+            r_out[a, h, 2 * SIZE :, :] = (value - value_hi.astype(jnp.float32)).astype(jnp.bfloat16)
         for k in range(1, parts):
             to = others[k]
-            sems = (ig_send.at[h, k], ig_recv.at[h, k])
-            returns.append(
-                remote(part(conv_out, to, size, h * size), part(ig_in, me, size, h * size), *sems, (section, to))
-            )
+            returns.append(remote(r_out.at[to, h], r_in.at[me, h], r_send.at[h, k], r_recv.at[h, k], (section, to)))
             returns[-1].start()
-            sems = (fg_send.at[h, k], fg_recv.at[h, k])
-            returns.append(
-                remote(part(corr, to, size, h * size), part(fg_in, me, size, h * size), *sems, (section, to))
-            )
-            returns[-1].start()
-    part(ig_in, me)[...] = part(conv_out, me)[...]
-    part(fg_in, me)[...] = part(corr, me)[...]
+    r_in[me] = r_out[me]
     for copy in returns:
         copy.wait_recv()
-    ig_ref[...] = ig_in[...].astype(jnp.float32).T.astype(jnp.bfloat16)
-    fg_ref[...] = fg_in[...].T
-    for copy in sends + returns:
+
+    def gathered(kind):
+        pieces = [
+            r_in[c, h, kind * SIZE : (kind + 1) * SIZE, :].astype(jnp.float32)
+            for c in range(parts)
+            for h in range(chunks)
+        ]
+        return jnp.concatenate(pieces, axis=0)
+
+    ig_ref[...] = gathered(0).T.astype(jnp.bfloat16)
+    fg_ref[...] = (gathered(1) + gathered(2)).T
+    for copy in sum(sends, returns):
         copy.wait_send()
 
 
 def kernel_per_device(pipes, parts, layer_input, filters, skip, incoming, loss_grad):
     rows, width = loss_grad.shape
+    chunks = width // parts // SIZE
     vmem = pl.BlockSpec(memory_space=pltpu.VMEM)
+    hbm = pl.BlockSpec(memory_space=pltpu.HBM)
     narrow = pltpu.VMEM((width, rows), jnp.bfloat16)
     wide = pltpu.VMEM((width, rows), jnp.float32)
-    padded = pltpu.VMEM((2 * width, rows), jnp.float32)
-    sems = [pltpu.SemaphoreType.DMA((parts,))] * 6 + [pltpu.SemaphoreType.DMA((2, parts))] * 4
+    triple = pltpu.VMEM((parts, chunks, 3 * SIZE, rows), jnp.bfloat16)
+    sems = pltpu.SemaphoreType.DMA((chunks, parts))
     input_grad, filter_grad = pl.pallas_call(
         functools.partial(correlate_kernel, pipes, parts),
         out_shape=(
             jax.ShapeDtypeStruct((rows, width), jnp.bfloat16),
             jax.ShapeDtypeStruct((rows, width), jnp.float32),
         ),
-        in_specs=[vmem, vmem, pl.BlockSpec(memory_space=pltpu.SMEM), vmem, vmem],
+        in_specs=[hbm] * 5,
         out_specs=(vmem, vmem),
-        scratch_shapes=[narrow, wide, narrow, narrow, narrow, padded, padded, wide, wide, wide, narrow, narrow, wide]
-        + sems,
+        scratch_shapes=[
+            pltpu.VMEM((rows, width), jnp.bfloat16),
+            pltpu.VMEM((rows, width), jnp.float32),
+            pltpu.VMEM((rows, width), jnp.bfloat16),
+            pltpu.SMEM((1, width), jnp.float32),
+            triple,
+            triple,
+            narrow,
+            narrow,
+            pltpu.VMEM((3, 2 * width, rows), jnp.float32),
+            wide,
+            wide,
+            wide,
+            triple,
+            triple,
+            pltpu.SemaphoreType.DMA((4,)),
+        ]
+        + [sems] * 6,
         compiler_params=pltpu.CompilerParams(
-            collective_id=0, has_side_effects=True, vmem_limit_bytes=32 * 1024 * 1024
+            collective_id=0, has_side_effects=True, vmem_limit_bytes=64 * 1024 * 1024 - 65536
         ),
     )(layer_input[0], filters[0], skip, incoming[0], loss_grad)
     return (input_grad[None], filter_grad[None])
@@ -273,7 +328,7 @@
 
     def step(layer_input, filters, skip, incoming, loss_grad):
         rows, width = loss_grad.shape
-        if pipes > 1 and parts == 8 and rows == 128 and width % (32 * parts) == 0:
+        if pipes > 1 and parts == 8 and rows == 128 and width % (2 * SIZE * parts) == 0:
             return kernel_per_device(pipes, parts, layer_input, filters, skip, incoming, loss_grad)
         return per_device(layer_input, filters, skip, incoming, loss_grad)
 

time: 33 us -> 26.8 us (0.81)
  local copies, waits for them, and re-layouts: 5.38 us -> 2.17 us
  Pallas kernels: 26.7 us -> 23.8 us
    unnamed x12 -> x4, local copies, waits for them, and re-layouts: 5.38 us -> 2.17 us
    pallas_call x1, Pallas kernels: 26.7 us -> 23.8 us  [kernel_per_device(): pl.pallas_call(functools.partial(correlate_kernel, pipes, parts), out_sha...]
where the time goes in v2:
time: 26.8 us; the launch traced here: 26.6 us
  Pallas kernels  23.8 us (89%)
  local copies, waits for them, and re-layouts  2.17 us (8%)
  between operations  0.65 us (2%)
    pallas_call x1, Pallas kernels, kernel_per_device(): pl.pallas_call(functools.partial(correlate_kernel, pipes, parts), out_sha...  23.8 us
    unnamed x4, local copies, waits for them, and re-layouts  2.17 us

profile of v2, /device:TPU:0, one launch (start us, length us, event | category | flops | bytes accessed | tf_op | source)
XLA Modules:
  0.0 26.6 jit_solution(11137411547580323871)
XLA Ops:
  0.6 23.8 %shard_map.68 = (bf16[128,256]{1,0:T(8,128)(2,1)}, f32[128,256]{1,0:T(8,128)}) custom-call(bf16[128,256]{1,0:T(8,128)(2,1)} %bitcast.7, f32[128,256]{1,0:T(8,128)} %bitcast.5, f32[1,256]{1,0:T(1,128)} %skip_hbm.1, bf16[128,256]{1,0:T(8,128)(2,1)} %bitcast.8, bf16[128,256]{1,0:T(8,128)(2,1)} %loss_hbm.1), custom_call_target="tpu_custom_call" | custom-call | tf_op jit(solution)/shard_map/pallas_call | solution.py:293
  24.4 0.0 copy-start
  24.4 1.5 %copy.9 = bf16[1,128,256]{2,1,0:T(8,128)(2,1)} copy(bf16[1,128,256]{2,1,0:T(8,128)(2,1)} %bitcast.9) | data formatting | bytes 131072
  25.9 0.0 copy-done
  25.9 0.7 %copy.10 = f32[1,128,256]{2,1,0:T(8,128)} copy(f32[1,128,256]{2,1,0:T(8,128)S(1)} %bitcast.6) | data formatting | bytes 262144
Async XLA Ops:
  24.4 1.5 %copy-start = (f32[128,256]{1,0:T(8,128)S(1)}, f32[128,256]{1,0:T(8,128)}, u32[]{:S(2)}) copy-start(f32[128,256]{1,0:T(8,128)} %get-tuple-element.5) | copy-start | bytes 393220

commit v3 on v2

--- a/solution.py
+++ b/solution.py
@@ -120,8 +120,8 @@
 
 
 def correlate_kernel(
-    pipes, parts, x_hbm, f_hbm, skip_hbm, inc_hbm, loss_hbm, ig_ref, fg_ref,
-    x_ref, f_ref, grad_ref, skip_ref, s_out, s_in, g_out, g_in, pads, g_val, conv, corr, r_out, r_in,
+    pipes, parts, x_hbm, f_hbm, skip_hbm, inc_hbm, loss_hbm, r_in,
+    x_ref, f_ref, grad_ref, skip_ref, s_out, s_in, g_out, g_in, pads, g_val, conv, corr, r_out,
     load_sem, s_send, s_recv, g_send, g_recv, r_send, r_recv,
 ):
     section = lax.axis_index("pipe")
@@ -267,9 +267,16 @@
     for copy in returns:
         copy.wait_recv()
 
+    for copy in sum(sends, returns):
+        copy.wait_send()
+
+
+def finish_kernel(r_ref, ig_ref, fg_ref):
+    parts, chunks = r_ref.shape[:2]
+
     def gathered(kind):
         pieces = [
-            r_in[c, h, kind * SIZE : (kind + 1) * SIZE, :].astype(jnp.float32)
+            r_ref[c, h, kind * SIZE : (kind + 1) * SIZE, :].astype(jnp.float32)
             for c in range(parts)
             for h in range(chunks)
         ]
@@ -277,27 +284,23 @@
 
     ig_ref[...] = gathered(0).T.astype(jnp.bfloat16)
     fg_ref[...] = (gathered(1) + gathered(2)).T
-    for copy in sum(sends, returns):
-        copy.wait_send()
 
 
 def kernel_per_device(pipes, parts, layer_input, filters, skip, incoming, loss_grad):
     rows, width = loss_grad.shape
     chunks = width // parts // SIZE
     vmem = pl.BlockSpec(memory_space=pltpu.VMEM)
-    hbm = pl.BlockSpec(memory_space=pltpu.HBM)
+    hbm = pl.BlockSpec(memory_space=pl.ANY)
     narrow = pltpu.VMEM((width, rows), jnp.bfloat16)
     wide = pltpu.VMEM((width, rows), jnp.float32)
     triple = pltpu.VMEM((parts, chunks, 3 * SIZE, rows), jnp.bfloat16)
     sems = pltpu.SemaphoreType.DMA((chunks, parts))
-    input_grad, filter_grad = pl.pallas_call(
+    operands = (layer_input[0], filters[0], skip, incoming[0], loss_grad)
+    returned = pl.pallas_call(
         functools.partial(correlate_kernel, pipes, parts),
-        out_shape=(
-            jax.ShapeDtypeStruct((rows, width), jnp.bfloat16),
-            jax.ShapeDtypeStruct((rows, width), jnp.float32),
-        ),
+        out_shape=pltpu.VMEM((parts, chunks, 3 * SIZE, rows), jnp.bfloat16),
         in_specs=[hbm] * 5,
-        out_specs=(vmem, vmem),
+        out_specs=vmem,
         scratch_shapes=[
             pltpu.VMEM((rows, width), jnp.bfloat16),
             pltpu.VMEM((rows, width), jnp.float32),
@@ -312,14 +315,22 @@
             wide,
             wide,
             triple,
-            triple,
             pltpu.SemaphoreType.DMA((4,)),
         ]
         + [sems] * 6,
         compiler_params=pltpu.CompilerParams(
-            collective_id=0, has_side_effects=True, vmem_limit_bytes=64 * 1024 * 1024 - 65536
+            collective_id=0, has_side_effects=True, vmem_limit_bytes=32 * 1024 * 1024
         ),
-    )(layer_input[0], filters[0], skip, incoming[0], loss_grad)
+    )(*[pltpu.with_memory_space_constraint(operand, pltpu.HBM) for operand in operands])
+    input_grad, filter_grad = pl.pallas_call(
+        finish_kernel,
+        out_shape=(
+            jax.ShapeDtypeStruct((rows, width), jnp.bfloat16),
+            jax.ShapeDtypeStruct((rows, width), jnp.float32),
+        ),
+        in_specs=[vmem],
+        out_specs=(vmem, vmem),
+    )(returned)
     return (input_grad[None], filter_grad[None])
 
 

time: 26.8 us -> 26.2 us (0.978)
  local copies, waits for them, and re-layouts: 2.17 us -> 0.66 us
  Pallas kernels: 23.8 us -> 24.7 us
    pallas_call x0 -> x1, Pallas kernels: none -> 1.72 us  [kernel_per_device(): pl.pallas_call(finish_kernel, out_shape=(jax.ShapeDtypeStruct((rows, widt...]
    unnamed x4 -> x2, local copies, waits for them, and re-layouts: 2.17 us -> 0.66 us
    pallas_call x1, Pallas kernels: 23.8 us -> 23 us  [kernel_per_device(): pl.pallas_call(functools.partial(correlate_kernel, pipes, parts), out_sha...]
where the time goes in v3:
time: 26.2 us; the launch traced here: 26 us
  Pallas kernels  24.7 us (94%)
  local copies, waits for them, and re-layouts  0.66 us (3%)
  between operations  0.65 us (2%)
    pallas_call x1, Pallas kernels, kernel_per_device(): pl.pallas_call(functools.partial(correlate_kernel, pipes, parts), out_sha...  23 us
    pallas_call x1, Pallas kernels, kernel_per_device(): pl.pallas_call(finish_kernel, out_shape=(jax.ShapeDtypeStruct((rows, widt...  1.72 us
    unnamed x2, local copies, waits for them, and re-layouts  0.66 us

profile of v3, /device:TPU:0, one launch (start us, length us, event | category | flops | bytes accessed | tf_op | source)
XLA Modules:
  0.0 26.0 jit_solution(4632165990131083912)
XLA Ops:
  0.6 23.0 %shard_map.68.r_ref = bf16[8,2,48,128]{3,2,1,0:T(8,128)(2,1)S(1)} custom-call(bf16[128,256]{1,0:T(8,128)(2,1)} %bitcast.6, f32[128,256]{1,0:T(8,128)} %bitcast.5, f32[1,256]{1,0:T(1,128)} %skip_hbm.1, bf16[128,256]{1,0:T(8,128)(2,1)} %bitcast.7, bf16[128,256]{1,0:T(8,128)(2,1)} %loss_hbm.1), custom_call_target="tpu_custom_call" | custom-call | tf_op jit(solution)/shard_map/pallas_call | solution.py:299
  23.6 0.0 copy-start
  23.6 0.7 %copy-done = bf16[8,2,48,128]{3,2,1,0:T(8,128)(2,1)} copy-done((bf16[8,2,48,128]{3,2,1,0:T(8,128)(2,1)}, bf16[8,2,48,128]{3,2,1,0:T(8,128)(2,1)S(1)}, u32[]{:S(2)}) %copy-start) | copy-done | bytes 196632
  24.3 1.7 %shard_map.69 = (bf16[128,256]{1,0:T(8,128)(2,1)}, f32[128,256]{1,0:T(8,128)}) custom-call(bf16[8,2,48,128]{3,2,1,0:T(8,128)(2,1)} %copy-done), custom_call_target="tpu_custom_call" | custom-call | tf_op jit(solution)/shard_map/pallas_call | solution.py:325
Async XLA Ops:
  23.6 0.7 %copy-start = (bf16[8,2,48,128]{3,2,1,0:T(8,128)(2,1)}, bf16[8,2,48,128]{3,2,1,0:T(8,128)(2,1)S(1)}, u32[]{:S(2)}) copy-start(bf16[8,2,48,128]{3,2,1,0:T(8,128)(2,1)S(1)} %shard_map.68.r_ref) | copy-start | bytes 589828

commit v4 on v3

--- a/solution.py
+++ b/solution.py
@@ -203,32 +203,36 @@
 
     keep = col_ids <= row_ids
 
-    def streams(kind, chan):
-        pieces = [
-            pads[kind, pl.ds((parts - 1 - e) * chans + chan, parts, stride=chans), :] for e in range(parts)
-        ]
-        return jnp.concatenate(pieces, axis=1)
-
-    def hankel(chan):
-        turned = []
-        for e in range(parts):
-            row = jnp.broadcast_to(g_val[pl.ds(e * chans + chan, 1), :], (rows, rows))
-            turned.append(pltpu.roll(row, 1, 1, stride=1, stride_axis=0))
-        turned.append(jnp.zeros((rows, rows), jnp.float32))
-        return jnp.concatenate(
-            [jnp.where(keep, turned[e], turned[e + 1]).astype(jnp.bfloat16) for e in range(parts)], axis=0
-        )
+    def stream(kind, chan, e):
+        return pads[kind, pl.ds((parts - 1 - e) * chans + chan, parts, stride=chans), :]
+
+    def turned(chan, e):
+        if e == parts:
+            return jnp.zeros((rows, rows), jnp.float32)
+        row = jnp.broadcast_to(g_val[pl.ds(e * chans + chan, 1), :], (rows, rows))
+        return pltpu.roll(row, 1, 1, stride=1, stride_axis=0)
 
     def pair(first):
-        left, right = [], []
-        for chan in (first, first + 1):
-            left += [streams(kind, chan) for kind in range(3)]
-            right.append(hankel(chan))
-        result = jnp.dot(
-            jnp.concatenate(left, axis=0).astype(jnp.bfloat16),
-            jnp.concatenate(right, axis=1),
-            preferred_element_type=jnp.float32,
-        )
+        both = (first, first + 1)
+        later = [turned(chan, 0) for chan in both]
+        result = jnp.zeros((6 * parts, 2 * rows), jnp.float32)
+        for start in range(0, parts, 2):
+            steps = (start, start + 1)
+            left = [
+                jnp.concatenate([stream(kind, chan, e) for e in steps], axis=1) for chan in both for kind in range(3)
+            ]
+            right = []
+            for e in steps:
+                blocks = []
+                for i in range(2):
+                    now, later[i] = later[i], turned(both[i], e + 1)
+                    blocks.append(jnp.where(keep, now, later[i]).astype(jnp.bfloat16))
+                right.append(jnp.concatenate(blocks, axis=1))
+            result += jnp.dot(
+                jnp.concatenate(left, axis=0).astype(jnp.bfloat16),
+                jnp.concatenate(right, axis=0),
+                preferred_element_type=jnp.float32,
+            )
         for i in range(2):
             chan = first + i
             mine = result[3 * parts * i : 3 * parts * (i + 1), rows * i : rows * (i + 1)]
@@ -251,7 +255,7 @@
             pair(h * SIZE + 2 * i)
             return carry
 
-        lax.fori_loop(0, SIZE // 2, body, 0, unroll=2)
+        lax.fori_loop(0, SIZE // 2, body, 0, unroll=4)
         for a in range(parts):
             held = slice(a * chans + h * SIZE, a * chans + (h + 1) * SIZE)
             value = corr[held, :]
@@ -271,7 +275,7 @@
         copy.wait_send()
 
 
-def finish_kernel(r_ref, ig_ref, fg_ref):
+def finish_kernel(r_ref, ig_hbm, fg_hbm, ig_ref, fg_ref, sems):
     parts, chunks = r_ref.shape[:2]
 
     def gathered(kind):
@@ -282,8 +286,14 @@
         ]
         return jnp.concatenate(pieces, axis=0)
 
+    store_fg = pltpu.make_async_copy(fg_ref, fg_hbm, sems.at[0])
+    store_ig = pltpu.make_async_copy(ig_ref, ig_hbm, sems.at[1])
+    fg_ref[...] = (gathered(1) + gathered(2)).T
+    store_fg.start()
     ig_ref[...] = gathered(0).T.astype(jnp.bfloat16)
-    fg_ref[...] = (gathered(1) + gathered(2)).T
+    store_ig.start()
+    store_fg.wait()
+    store_ig.wait()
 
 
 def kernel_per_device(pipes, parts, layer_input, filters, skip, incoming, loss_grad):
@@ -329,7 +339,13 @@
             jax.ShapeDtypeStruct((rows, width), jnp.float32),
         ),
         in_specs=[vmem],
-        out_specs=(vmem, vmem),
+        out_specs=(hbm, hbm),
+        scratch_shapes=[
+            pltpu.VMEM((rows, width), jnp.bfloat16),
+            pltpu.VMEM((rows, width), jnp.float32),
+            pltpu.SemaphoreType.DMA((2,)),
+        ],
+        compiler_params=pltpu.CompilerParams(vmem_limit_bytes=8 * 1024 * 1024),
     )(returned)
     return (input_grad[None], filter_grad[None])
 

time: 26.2 us -> 24 us (0.916)
  Pallas kernels: 24.7 us -> 23.2 us
  local copies, waits for them, and re-layouts: 0.66 us -> 0 us
    pallas_call x1, Pallas kernels: 1.72 us -> 0.79 us  [kernel_per_device(): pl.pallas_call(finish_kernel, out_shape=(jax.ShapeDtypeStruct((rows, widt...]
    unnamed x2 -> x0, local copies, waits for them, and re-layouts: 0.66 us -> none
    pallas_call x1, Pallas kernels: 23 us -> 22.4 us  [kernel_per_device(): pl.pallas_call(functools.partial(correlate_kernel, pipes, parts), out_sha...]
where the time goes in v4:
time: 24 us; the launch traced here: 23.8 us
  Pallas kernels  23.2 us (97%)
  between operations  0.64 us (3%)
    pallas_call x1, Pallas kernels, kernel_per_device(): pl.pallas_call(functools.partial(correlate_kernel, pipes, parts), out_sha...  22.4 us
    pallas_call x1, Pallas kernels, kernel_per_device(): pl.pallas_call(finish_kernel, out_shape=(jax.ShapeDtypeStruct((rows, widt...  0.79 us

profile of v4, /device:TPU:0, one launch (start us, length us, event | category | flops | bytes accessed | tf_op | source)
XLA Modules:
  0.0 23.8 jit_solution(11544919492238495888)
XLA Ops:
  0.6 22.4 %shard_map.68.r_ref = bf16[8,2,48,128]{3,2,1,0:T(8,128)(2,1)S(1)} custom-call(bf16[128,256]{1,0:T(8,128)(2,1)} %bitcast.6, f32[128,256]{1,0:T(8,128)} %bitcast.5, f32[1,256]{1,0:T(1,128)} %skip_hbm.1, bf16[128,256]{1,0:T(8,128)(2,1)} %bitcast.7, bf16[128,256]{1,0:T(8,128)(2,1)} %loss_hbm.1), custom_call_target="tpu_custom_call" | custom-call | tf_op jit(solution)/shard_map/pallas_call | solution.py:309
  23.0 0.8 %shard_map.69 = (bf16[128,256]{1,0:T(8,128)(2,1)}, f32[128,256]{1,0:T(8,128)}) custom-call(bf16[8,2,48,128]{3,2,1,0:T(8,128)(2,1)S(1)} %shard_map.68.r_ref), custom_call_target="tpu_custom_call" | custom-call | tf_op jit(solution)/shard_map/pallas_call | solution.py:335

commit v5 on v4

--- a/solution.py
+++ b/solution.py
@@ -208,8 +208,8 @@
 
     def turned(chan, e):
         if e == parts:
-            return jnp.zeros((rows, rows), jnp.float32)
-        row = jnp.broadcast_to(g_val[pl.ds(e * chans + chan, 1), :], (rows, rows))
+            return jnp.zeros((rows, rows), jnp.bfloat16)
+        row = jnp.broadcast_to(g_val[pl.ds(e * chans + chan, 1), :].astype(jnp.bfloat16), (rows, rows))
         return pltpu.roll(row, 1, 1, stride=1, stride_axis=0)
 
     def pair(first):
@@ -226,7 +226,7 @@
                 blocks = []
                 for i in range(2):
                     now, later[i] = later[i], turned(both[i], e + 1)
-                    blocks.append(jnp.where(keep, now, later[i]).astype(jnp.bfloat16))
+                    blocks.append(jnp.where(keep, now, later[i]))
                 right.append(jnp.concatenate(blocks, axis=1))
             result += jnp.dot(
                 jnp.concatenate(left, axis=0).astype(jnp.bfloat16),

time: 24 us -> 23.3 us (0.971)
  Pallas kernels: 23.2 us -> 22.5 us
    pallas_call x1, Pallas kernels: 22.4 us -> 21.7 us  [kernel_per_device(): pl.pallas_call(functools.partial(correlate_kernel, pipes, parts), out_sha...]
where the time goes in v5:
time: 23.3 us; the launch traced here: 23.2 us
  Pallas kernels  22.5 us (97%)
  between operations  0.64 us (3%)
    pallas_call x1, Pallas kernels, kernel_per_device(): pl.pallas_call(functools.partial(correlate_kernel, pipes, parts), out_sha...  21.7 us
    pallas_call x1, Pallas kernels, kernel_per_device(): pl.pallas_call(finish_kernel, out_shape=(jax.ShapeDtypeStruct((rows, widt...  0.79 us

profile of v5, /device:TPU:0, one launch (start us, length us, event | category | flops | bytes accessed | tf_op | source)
XLA Modules:
  0.0 23.2 jit_solution(12879621736497532241)
XLA Ops:
  0.6 21.7 %shard_map.68.r_ref = bf16[8,2,48,128]{3,2,1,0:T(8,128)(2,1)S(1)} custom-call(bf16[128,256]{1,0:T(8,128)(2,1)} %bitcast.6, f32[128,256]{1,0:T(8,128)} %bitcast.5, f32[1,256]{1,0:T(1,128)} %skip_hbm.1, bf16[128,256]{1,0:T(8,128)(2,1)} %bitcast.7, bf16[128,256]{1,0:T(8,128)(2,1)} %loss_hbm.1), custom_call_target="tpu_custom_call" | custom-call | tf_op jit(solution)/shard_map/pallas_call | solution.py:309
  22.4 0.8 %shard_map.69 = (bf16[128,256]{1,0:T(8,128)(2,1)}, f32[128,256]{1,0:T(8,128)}) custom-call(bf16[8,2,48,128]{3,2,1,0:T(8,128)(2,1)S(1)} %shard_map.68.r_ref), custom_call_target="tpu_custom_call" | custom-call | tf_op jit(solution)/shard_map/pallas_call | solution.py:335

commit v6 on v5

--- a/solution.py
+++ b/solution.py
@@ -111,6 +111,7 @@
 
 
 SIZE = 16
+FINE = 32
 
 
 def remote(src, dst, send_sem, recv_sem, device):
@@ -157,8 +158,6 @@
     row_ids = lax.broadcasted_iota(jnp.int32, (rows, rows), 0)
     col_ids = lax.broadcasted_iota(jnp.int32, (rows, rows), 1)
     flip = jnp.where(row_ids + col_ids == rows - 1, 1.0, 0.0).astype(jnp.bfloat16)
-    for kind in range(3):
-        pads[kind, parts * chans :, :] = jnp.zeros((parts * chans, rows), jnp.float32)
 
     def turned_over(block):
         return jnp.dot(flip, block, preferred_element_type=jnp.float32).T.astype(jnp.bfloat16)
@@ -201,45 +200,72 @@
     s_in[slot] = s_out[me]
     load_skip.wait()
 
-    keep = col_ids <= row_ids
-
-    def stream(kind, chan, e):
-        return pads[kind, pl.ds((parts - 1 - e) * chans + chan, parts, stride=chans), :]
+    groups = rows // FINE
+    lane = lax.broadcasted_iota(jnp.int32, (3 * SIZE, rows), 1) // FINE
+    fine_row = lax.broadcasted_iota(jnp.int32, (FINE, rows), 0)
+    fine_col = lax.broadcasted_iota(jnp.int32, (FINE, rows), 1)
+    keep = fine_col + FINE - 1 - fine_row < rows
+    wide_lane = lax.broadcasted_iota(jnp.int32, (parts, rows), 1)
+    tiles = parts // groups
+
+    def spread(h):
+        nothing = jnp.zeros((3 * SIZE, rows), jnp.bfloat16)
+        turns = []
+        for e in range(parts):
+            block = s_in[e, h]
+            turns.append([block] + [pltpu.roll(block, FINE * r, 1) for r in range(1, groups)])
+        for j in range(groups):
+            for a in range(parts):
+                for v in range(tiles):
+                    value = nothing
+                    for q in range(groups):
+                        e = groups * v + q + a
+                        if e < parts:
+                            value = jnp.where(lane == q, turns[e][(q - j) % groups], value)
+                    value = value.astype(jnp.float32)
+                    for kind in range(3):
+                        start = ((kind * groups + j) * parts + a) * SIZE
+                        pads[v, start : start + SIZE, :] = value[kind * SIZE : (kind + 1) * SIZE]
 
     def turned(chan, e):
-        if e == parts:
-            return jnp.zeros((rows, rows), jnp.bfloat16)
-        row = jnp.broadcast_to(g_val[pl.ds(e * chans + chan, 1), :].astype(jnp.bfloat16), (rows, rows))
-        return pltpu.roll(row, 1, 1, stride=1, stride_axis=0)
-
-    def pair(first):
-        both = (first, first + 1)
-        later = [turned(chan, 0) for chan in both]
-        result = jnp.zeros((6 * parts, 2 * rows), jnp.float32)
-        for start in range(0, parts, 2):
-            steps = (start, start + 1)
-            left = [
-                jnp.concatenate([stream(kind, chan, e) for e in steps], axis=1) for chan in both for kind in range(3)
-            ]
-            right = []
-            for e in steps:
-                blocks = []
-                for i in range(2):
-                    now, later[i] = later[i], turned(both[i], e + 1)
-                    blocks.append(jnp.where(keep, now, later[i]))
-                right.append(jnp.concatenate(blocks, axis=1))
-            result += jnp.dot(
-                jnp.concatenate(left, axis=0).astype(jnp.bfloat16),
-                jnp.concatenate(right, axis=0),
-                preferred_element_type=jnp.float32,
-            )
-        for i in range(2):
-            chan = first + i
-            mine = result[3 * parts * i : 3 * parts * (i + 1), rows * i : rows * (i + 1)]
-            where = pl.ds(chan, parts, stride=chans)
-            gain = skip_ref[0, me * chans + chan]
-            conv[where, :] = mine[:parts] + mine[parts : 2 * parts] + gain * g_val[where, :]
-            corr[where, :] = mine[2 * parts :] * (1.0 / math.sqrt(rows * parts))
+        row = jnp.broadcast_to(g_val[pl.ds(e * chans + chan, 1), :].astype(jnp.bfloat16), (FINE, rows))
+        return pltpu.roll(row, rows - FINE + 1, 1, stride=1, stride_axis=0)
+
+    def one(h, i):
+        chan = h * SIZE + i
+        nothing = jnp.zeros((FINE, rows), jnp.bfloat16)
+        turns = [turned(chan, e) for e in range(parts)] + [nothing]
+        blocks = [jnp.where(keep, turns[e], turns[e + 1]) for e in range(parts)] + [nothing]
+        right = jnp.concatenate(
+            [jnp.concatenate([blocks[e], blocks[e + 1]], axis=1) for e in reversed(range(parts))], axis=0
+        )
+        left = jnp.concatenate(
+            [
+                jnp.concatenate(
+                    [pads[v, pl.ds(m * parts * SIZE + i, parts, stride=SIZE), :] for v in range(tiles)], axis=1
+                )
+                for m in range(3 * groups)
+            ],
+            axis=0,
+        )
+        result = jnp.dot(left.astype(jnp.bfloat16), right, preferred_element_type=jnp.float32)
+
+        def folded(kinds):
+            total = None
+            for j in range(groups):
+                begin = FINE * (groups - 1 - j)
+                part = sum(result[(kind * groups + j) * parts : (kind * groups + j + 1) * parts] for kind in kinds)
+                piece = part[:, :rows]
+                if begin:
+                    piece = jnp.where(wide_lane >= begin, piece, part[:, rows:])
+                    piece = pltpu.roll(piece, rows - begin, 1)
+                total = piece if total is None else total + piece
+            return total
+
+        where = pl.ds(chan, parts, stride=chans)
+        gain = skip_ref[0, me * chans + chan]
+        conv[where, :] = folded((0, 1)) + gain * g_val[where, :]
+        corr[where, :] = folded((2,)) * (1.0 / math.sqrt(rows * parts))
 
     returns = []
     for h in range(chunks):
@@ -248,14 +274,13 @@
         for e in range(parts):
             held = slice(e * chans + h * SIZE, e * chans + (h + 1) * SIZE)
             g_val[held, :] = g_in[held, :].astype(jnp.float32)
-            for kind in range(3):
-                pads[kind, held, :] = s_in[e, h, kind * SIZE : (kind + 1) * SIZE, :].astype(jnp.float32)
+        spread(h)
 
         def body(i, carry):
-            pair(h * SIZE + 2 * i)
+            one(h, i)
             return carry
 
-        lax.fori_loop(0, SIZE // 2, body, 0, unroll=4)
+        lax.fori_loop(0, SIZE, body, 0, unroll=8)
         for a in range(parts):
             held = slice(a * chans + h * SIZE, a * chans + (h + 1) * SIZE)
             value = corr[held, :]
@@ -320,7 +345,7 @@
             triple,
             narrow,
             narrow,
-            pltpu.VMEM((3, 2 * width, rows), jnp.float32),
+            pltpu.VMEM((parts * FINE // rows, 3 * (rows // FINE) * parts * SIZE, rows), jnp.float32),
             wide,
             wide,
             wide,

time: 23.3 us -> 22.2 us (0.953)
  Pallas kernels: 22.5 us -> 21.4 us
    pallas_call x1, Pallas kernels: 21.7 us -> 20.6 us  [kernel_per_device(): pl.pallas_call(functools.partial(correlate_kernel, pipes, parts), out_sha...]
where the time goes in v6:
time: 22.2 us; the launch traced here: 22.1 us
  Pallas kernels  21.4 us (96%)
  between operations  0.64 us (3%)
    pallas_call x1, Pallas kernels, kernel_per_device(): pl.pallas_call(functools.partial(correlate_kernel, pipes, parts), out_sha...  20.6 us
    pallas_call x1, Pallas kernels, kernel_per_device(): pl.pallas_call(finish_kernel, out_shape=(jax.ShapeDtypeStruct((rows, widt...  0.79 us

profile of v6, /device:TPU:0, one launch (start us, length us, event | category | flops | bytes accessed | tf_op | source)
XLA Modules:
  0.0 22.1 jit_solution(15542047643486376780)
XLA Ops:
  0.6 20.6 %shard_map.68.r_ref = bf16[8,2,48,128]{3,2,1,0:T(8,128)(2,1)S(1)} custom-call(bf16[128,256]{1,0:T(8,128)(2,1)} %bitcast.6, f32[128,256]{1,0:T(8,128)} %bitcast.5, f32[1,256]{1,0:T(1,128)} %skip_hbm.1, bf16[128,256]{1,0:T(8,128)(2,1)} %bitcast.7, bf16[128,256]{1,0:T(8,128)(2,1)} %loss_hbm.1), custom_call_target="tpu_custom_call" | custom-call | tf_op jit(solution)/shard_map/pallas_call | solution.py:334
  21.3 0.8 %shard_map.69 = (bf16[128,256]{1,0:T(8,128)(2,1)}, f32[128,256]{1,0:T(8,128)}) custom-call(bf16[8,2,48,128]{3,2,1,0:T(8,128)(2,1)S(1)} %shard_map.68.r_ref), custom_call_target="tpu_custom_call" | custom-call | tf_op jit(solution)/shard_map/pallas_call | solution.py:360

commit v7 on v6

--- a/solution.py
+++ b/solution.py
@@ -155,6 +155,25 @@
             pl.semaphore_signal(barrier, inc=1, device_id=(section, others[k]), device_id_type=MESH)
         pl.semaphore_signal(barrier, inc=1, device_id=(after, others[k]), device_id_type=MESH)
 
+    far_first = sorted(range(1, parts), key=lambda k: abs(k - parts // 2))
+    slot = parts - 1 - me
+
+    def block_of(index):
+        return pl.ds(pl.multiple_of(index * chans, SIZE), chans)
+
+    pltpu.make_async_copy(inc_hbm, grad_ref, load_sem.at[0]).wait()
+    g_out[...] = grad_ref[...].astype(jnp.float32).T.astype(jnp.bfloat16)
+
+    pl.semaphore_wait(barrier, 2 * parts - 1)
+
+    g_sends = []
+    for k in far_first + [0]:
+        to = others[k]
+        g_sends.append(
+            remote(g_out.at[block_of(to)], g_in.at[block_of(me)], g_send.at[k], g_recv.at[k], (before, to))
+        )
+        g_sends[-1].start()
+
     row_ids = lax.broadcasted_iota(jnp.int32, (rows, rows), 0)
     col_ids = lax.broadcasted_iota(jnp.int32, (rows, rows), 1)
     flip = jnp.where(row_ids + col_ids == rows - 1, 1.0, 0.0).astype(jnp.bfloat16)
@@ -168,8 +187,6 @@
                 start = c * chans + h * SIZE
                 s_out[c, h, kind * SIZE : (kind + 1) * SIZE, :] = block[start : start + SIZE]
 
-    pltpu.make_async_copy(inc_hbm, grad_ref, load_sem.at[0]).wait()
-    g_out[...] = grad_ref[...].astype(jnp.float32).T.astype(jnp.bfloat16)
     load_f.wait()
     filt = f_ref[...]
     filt_hi = filt.astype(jnp.bfloat16)
@@ -178,27 +195,20 @@
     load_x.wait()
     place(2, turned_over(x_ref[...]))
 
-    pl.semaphore_wait(barrier, 2 * parts - 1)
-
-    def span(index, h):
-        return pl.ds(pl.multiple_of(index * chans + h * SIZE, SIZE), SIZE)
-
-    slot = parts - 1 - me
     sends = []
     for h in range(chunks):
         group = []
-        for k in range(parts):
+        for k in far_first:
             to = others[k]
-            sems = (g_send.at[h, k], g_recv.at[h, k])
-            group.append(remote(g_out.at[span(to, h)], g_in.at[span(me, h)], *sems, (before, to)))
+            sems = (s_send.at[h, k], s_recv.at[h, k])
+            group.append(remote(s_out.at[to, h], s_in.at[slot, h], *sems, (section, to)))
             group[-1].start()
-            if k:
-                sems = (s_send.at[h, k], s_recv.at[h, k])
-                group.append(remote(s_out.at[to, h], s_in.at[slot, h], *sems, (section, to)))
-                group[-1].start()
         sends.append(group)
     s_in[slot] = s_out[me]
     load_skip.wait()
+    for copy in g_sends:
+        copy.wait_recv()
+    g_val[...] = g_in[...].astype(jnp.float32)
 
     groups = rows // FINE
     lane = lax.broadcasted_iota(jnp.int32, (3 * SIZE, rows), 1) // FINE
@@ -271,9 +281,6 @@
     for h in range(chunks):
         for copy in sends[h]:
             copy.wait_recv()
-        for e in range(parts):
-            held = slice(e * chans + h * SIZE, e * chans + (h + 1) * SIZE)
-            g_val[held, :] = g_in[held, :].astype(jnp.float32)
         spread(h)
 
         def body(i, carry):
@@ -288,7 +295,7 @@
             r_out[a, h, :SIZE, :] = conv[held, :].astype(jnp.bfloat16)
             r_out[a, h, SIZE : 2 * SIZE, :] = value_hi
             r_out[a, h, 2 * SIZE :, :] = (value - value_hi.astype(jnp.float32)).astype(jnp.bfloat16)
-        for k in range(1, parts):
+        for k in far_first:
             to = others[k]
             returns.append(remote(r_out.at[to, h], r_in.at[me, h], r_send.at[h, k], r_recv.at[h, k], (section, to)))
             returns[-1].start()
@@ -296,7 +303,7 @@
     for copy in returns:
         copy.wait_recv()
 
-    for copy in sum(sends, returns):
+    for copy in sum(sends, g_sends + returns):
         copy.wait_send()
 
 
@@ -352,7 +359,9 @@
             triple,
             pltpu.SemaphoreType.DMA((4,)),
         ]
-        + [sems] * 6,
+        + [sems] * 2
+        + [pltpu.SemaphoreType.DMA((parts,))] * 2
+        + [sems] * 2,
         compiler_params=pltpu.CompilerParams(
             collective_id=0, has_side_effects=True, vmem_limit_bytes=32 * 1024 * 1024
         ),

time: 22.2 us -> 23.2 us (1.045)
  Pallas kernels: 21.4 us -> 22.5 us
    pallas_call x1, Pallas kernels: 20.6 us -> 21.7 us  [kernel_per_device(): pl.pallas_call(functools.partial(correlate_kernel, pipes, parts), out_sha...]
where the time goes in v7:
time: 23.2 us; the launch traced here: 23.1 us
  Pallas kernels  22.5 us (97%)
  between operations  0.64 us (3%)
    pallas_call x1, Pallas kernels, kernel_per_device(): pl.pallas_call(functools.partial(correlate_kernel, pipes, parts), out_sha...  21.7 us
    pallas_call x1, Pallas kernels, kernel_per_device(): pl.pallas_call(finish_kernel, out_shape=(jax.ShapeDtypeStruct((rows, widt...  0.79 us

profile of v7, /device:TPU:0, one launch (start us, length us, event | category | flops | bytes accessed | tf_op | source)
XLA Modules:
  0.0 23.1 jit_solution(17402999695851116559)
XLA Ops:
  0.6 21.7 %shard_map.68.r_ref = bf16[8,2,48,128]{3,2,1,0:T(8,128)(2,1)S(1)} custom-call(bf16[128,256]{1,0:T(8,128)(2,1)} %bitcast.6, f32[128,256]{1,0:T(8,128)} %bitcast.5, f32[1,256]{1,0:T(1,128)} %skip_hbm.1, bf16[128,256]{1,0:T(8,128)(2,1)} %bitcast.7, bf16[128,256]{1,0:T(8,128)(2,1)} %loss_hbm.1), custom_call_target="tpu_custom_call" | custom-call | tf_op jit(solution)/shard_map/pallas_call | solution.py:341
  22.3 0.8 %shard_map.69 = (bf16[128,256]{1,0:T(8,128)(2,1)}, f32[128,256]{1,0:T(8,128)}) custom-call(bf16[8,2,48,128]{3,2,1,0:T(8,128)(2,1)S(1)} %shard_map.68.r_ref), custom_call_target="tpu_custom_call" | custom-call | tf_op jit(solution)/shard_map/pallas_call | solution.py:369

commit v8 on v7

--- a/solution.py
+++ b/solution.py
@@ -155,7 +155,6 @@
             pl.semaphore_signal(barrier, inc=1, device_id=(section, others[k]), device_id_type=MESH)
         pl.semaphore_signal(barrier, inc=1, device_id=(after, others[k]), device_id_type=MESH)
 
-    far_first = sorted(range(1, parts), key=lambda k: abs(k - parts // 2))
     slot = parts - 1 - me
 
     def block_of(index):
@@ -163,16 +162,6 @@
 
     pltpu.make_async_copy(inc_hbm, grad_ref, load_sem.at[0]).wait()
     g_out[...] = grad_ref[...].astype(jnp.float32).T.astype(jnp.bfloat16)
-
-    pl.semaphore_wait(barrier, 2 * parts - 1)
-
-    g_sends = []
-    for k in far_first + [0]:
-        to = others[k]
-        g_sends.append(
-            remote(g_out.at[block_of(to)], g_in.at[block_of(me)], g_send.at[k], g_recv.at[k], (before, to))
-        )
-        g_sends[-1].start()
 
     row_ids = lax.broadcasted_iota(jnp.int32, (rows, rows), 0)
     col_ids = lax.broadcasted_iota(jnp.int32, (rows, rows), 1)
@@ -195,14 +184,21 @@
     load_x.wait()
     place(2, turned_over(x_ref[...]))
 
-    sends = []
+    pl.semaphore_wait(barrier, 2 * parts - 1)
+
+    sends, g_sends = [], []
     for h in range(chunks):
         group = []
-        for k in far_first:
-            to = others[k]
-            sems = (s_send.at[h, k], s_recv.at[h, k])
-            group.append(remote(s_out.at[to, h], s_in.at[slot, h], *sems, (section, to)))
-            group[-1].start()
+        for k in range(1, parts + 1):
+            to = others[k % parts]
+            if k < parts:
+                sems = (s_send.at[h, k], s_recv.at[h, k])
+                group.append(remote(s_out.at[to, h], s_in.at[slot, h], *sems, (section, to)))
+                group[-1].start()
+            if h == 0:
+                sems = (g_send.at[k % parts], g_recv.at[k % parts])
+                g_sends.append(remote(g_out.at[block_of(to)], g_in.at[block_of(me)], *sems, (before, to)))
+                g_sends[-1].start()
         sends.append(group)
     s_in[slot] = s_out[me]
     load_skip.wait()
@@ -295,7 +291,7 @@
             r_out[a, h, :SIZE, :] = conv[held, :].astype(jnp.bfloat16)
             r_out[a, h, SIZE : 2 * SIZE, :] = value_hi
             r_out[a, h, 2 * SIZE :, :] = (value - value_hi.astype(jnp.float32)).astype(jnp.bfloat16)
-        for k in far_first:
+        for k in range(1, parts):
             to = others[k]
             returns.append(remote(r_out.at[to, h], r_in.at[me, h], r_send.at[h, k], r_recv.at[h, k], (section, to)))
             returns[-1].start()

time: 23.2 us -> 22.4 us (0.966)
  Pallas kernels: 22.5 us -> 21.6 us
    pallas_call x1, Pallas kernels: 21.7 us -> 20.8 us  [kernel_per_device(): pl.pallas_call(functools.partial(correlate_kernel, pipes, parts), out_sha...]
where the time goes in v8:
time: 22.4 us; the launch traced here: 22.2 us
  Pallas kernels  21.6 us (96%)
  between operations  0.64 us (3%)
    pallas_call x1, Pallas kernels, kernel_per_device(): pl.pallas_call(functools.partial(correlate_kernel, pipes, parts), out_sha...  20.8 us
    pallas_call x1, Pallas kernels, kernel_per_device(): pl.pallas_call(finish_kernel, out_shape=(jax.ShapeDtypeStruct((rows, widt...  0.79 us

profile of v8, /device:TPU:0, one launch (start us, length us, event | category | flops | bytes accessed | tf_op | source)
XLA Modules:
  0.0 22.2 jit_solution(1935558868178623026)
XLA Ops:
  0.6 20.8 %shard_map.68.r_ref = bf16[8,2,48,128]{3,2,1,0:T(8,128)(2,1)S(1)} custom-call(bf16[128,256]{1,0:T(8,128)(2,1)} %bitcast.6, f32[128,256]{1,0:T(8,128)} %bitcast.5, f32[1,256]{1,0:T(1,128)} %skip_hbm.1, bf16[128,256]{1,0:T(8,128)(2,1)} %bitcast.7, bf16[128,256]{1,0:T(8,128)(2,1)} %loss_hbm.1), custom_call_target="tpu_custom_call" | custom-call | tf_op jit(solution)/shard_map/pallas_call | solution.py:337
  21.4 0.8 %shard_map.69 = (bf16[128,256]{1,0:T(8,128)(2,1)}, f32[128,256]{1,0:T(8,128)}) custom-call(bf16[8,2,48,128]{3,2,1,0:T(8,128)(2,1)S(1)} %shard_map.68.r_ref), custom_call_target="tpu_custom_call" | custom-call | tf_op jit(solution)/shard_map/pallas_call | solution.py:365

commit v9 on v6

--- a/solution.py
+++ b/solution.py
@@ -187,6 +187,8 @@
     sends = []
     for h in range(chunks):
         group = []
+        for copy in sum(sends, []):
+            copy.wait_send()
         for k in range(parts):
             to = others[k]
             sems = (g_send.at[h, k], g_recv.at[h, k])
@@ -296,7 +298,7 @@
     for copy in returns:
         copy.wait_recv()
 
-    for copy in sum(sends, returns):
+    for copy in sends[-1] + returns:
         copy.wait_send()
 
 

time: 22.2 us -> 22.2 us (level)
  no operation moved by 1% of the time
where the time goes in v9:
time: 22.2 us; the launch traced here: 22 us
  Pallas kernels  21.4 us (96%)
  between operations  0.64 us (3%)
    pallas_call x1, Pallas kernels, kernel_per_device(): pl.pallas_call(functools.partial(correlate_kernel, pipes, parts), out_sha...  20.6 us
    pallas_call x1, Pallas kernels, kernel_per_device(): pl.pallas_call(finish_kernel, out_shape=(jax.ShapeDtypeStruct((rows, widt...  0.79 us

profile of v9, /device:TPU:0, one launch (start us, length us, event | category | flops | bytes accessed | tf_op | source)
XLA Modules:
  0.0 22.0 jit_solution(12743186343056534545)
XLA Ops:
  0.6 20.6 %shard_map.68.r_ref = bf16[8,2,48,128]{3,2,1,0:T(8,128)(2,1)S(1)} custom-call(bf16[128,256]{1,0:T(8,128)(2,1)} %bitcast.6, f32[128,256]{1,0:T(8,128)} %bitcast.5, f32[1,256]{1,0:T(1,128)} %skip_hbm.1, bf16[128,256]{1,0:T(8,128)(2,1)} %bitcast.7, bf16[128,256]{1,0:T(8,128)(2,1)} %loss_hbm.1), custom_call_target="tpu_custom_call" | custom-call | tf_op jit(solution)/shard_map/pallas_call | solution.py:336
  21.2 0.8 %shard_map.69 = (bf16[128,256]{1,0:T(8,128)(2,1)}, f32[128,256]{1,0:T(8,128)}) custom-call(bf16[8,2,48,128]{3,2,1,0:T(8,128)(2,1)S(1)} %shard_map.68.r_ref), custom_call_target="tpu_custom_call" | custom-call | tf_op jit(solution)/shard_map/pallas_call | solution.py:362

commit v10 on v6

--- a/solution.py
+++ b/solution.py
@@ -160,7 +160,7 @@
     flip = jnp.where(row_ids + col_ids == rows - 1, 1.0, 0.0).astype(jnp.bfloat16)
 
     def turned_over(block):
-        return jnp.dot(flip, block, preferred_element_type=jnp.float32).T.astype(jnp.bfloat16)
+        return jnp.dot(flip, block, preferred_element_type=jnp.float32).astype(jnp.bfloat16).T
 
     def place(kind, block):
         for c in range(parts):
@@ -169,7 +169,7 @@
                 s_out[c, h, kind * SIZE : (kind + 1) * SIZE, :] = block[start : start + SIZE]
 
     pltpu.make_async_copy(inc_hbm, grad_ref, load_sem.at[0]).wait()
-    g_out[...] = grad_ref[...].astype(jnp.float32).T.astype(jnp.bfloat16)
+    g_out[...] = grad_ref[...].T
     load_f.wait()
     filt = f_ref[...]
     filt_hi = filt.astype(jnp.bfloat16)
@@ -280,7 +280,7 @@
             one(h, i)
             return carry
 
-        lax.fori_loop(0, SIZE, body, 0, unroll=8)
+        lax.fori_loop(0, SIZE, body, 0, unroll=16)
         for a in range(parts):
             held = slice(a * chans + h * SIZE, a * chans + (h + 1) * SIZE)
             value = corr[held, :]
@@ -305,7 +305,7 @@
 
     def gathered(kind):
         pieces = [
-            r_ref[c, h, kind * SIZE : (kind + 1) * SIZE, :].astype(jnp.float32)
+            r_ref[c, h, kind * SIZE : (kind + 1) * SIZE, :]
             for c in range(parts)
             for h in range(chunks)
         ]
@@ -313,9 +313,9 @@
 
     store_fg = pltpu.make_async_copy(fg_ref, fg_hbm, sems.at[0])
     store_ig = pltpu.make_async_copy(ig_ref, ig_hbm, sems.at[1])
-    fg_ref[...] = (gathered(1) + gathered(2)).T
+    fg_ref[...] = (gathered(1).astype(jnp.float32) + gathered(2).astype(jnp.float32)).T
     store_fg.start()
-    ig_ref[...] = gathered(0).T.astype(jnp.bfloat16)
+    ig_ref[...] = gathered(0).T
     store_ig.start()
     store_fg.wait()
     store_ig.wait()

time: 22.2 us -> 21.8 us (0.982)
  Pallas kernels: 21.4 us -> 21.1 us
    pallas_call x1, Pallas kernels: 20.6 us -> 20.3 us  [kernel_per_device(): pl.pallas_call(functools.partial(correlate_kernel, pipes, parts), out_sha...]
where the time goes in v10:
time: 21.8 us; the launch traced here: 21.7 us
  Pallas kernels  21.1 us (97%)
  between operations  0.64 us (3%)
    pallas_call x1, Pallas kernels, kernel_per_device(): pl.pallas_call(functools.partial(correlate_kernel, pipes, parts), out_sha...  20.3 us
    pallas_call x1, Pallas kernels, kernel_per_device(): pl.pallas_call(finish_kernel, out_shape=(jax.ShapeDtypeStruct((rows, widt...  0.79 us

profile of v10, /device:TPU:0, one launch (start us, length us, event | category | flops | bytes accessed | tf_op | source)
XLA Modules:
  0.0 21.7 jit_solution(11393967571280028476)
XLA Ops:
  0.6 20.3 %shard_map.68.r_ref = bf16[8,2,48,128]{3,2,1,0:T(8,128)(2,1)S(1)} custom-call(bf16[128,256]{1,0:T(8,128)(2,1)} %bitcast.6, f32[128,256]{1,0:T(8,128)} %bitcast.5, f32[1,256]{1,0:T(1,128)} %skip_hbm.1, bf16[128,256]{1,0:T(8,128)(2,1)} %bitcast.7, bf16[128,256]{1,0:T(8,128)(2,1)} %loss_hbm.1), custom_call_target="tpu_custom_call" | custom-call | tf_op jit(solution)/shard_map/pallas_call | solution.py:334
  20.9 0.8 %shard_map.69 = (bf16[128,256]{1,0:T(8,128)(2,1)}, f32[128,256]{1,0:T(8,128)}) custom-call(bf16[8,2,48,128]{3,2,1,0:T(8,128)(2,1)S(1)} %shard_map.68.r_ref), custom_call_target="tpu_custom_call" | custom-call | tf_op jit(solution)/shard_map/pallas_call | solution.py:360

commit v11 on v10

--- a/solution.py
+++ b/solution.py
@@ -132,7 +132,8 @@
     chunks = chans // SIZE
     before = lax.rem(section + pipes - 1, pipes)
     after = lax.rem(section + 1, pipes)
-    others = [lax.rem(me + k, parts) for k in range(parts)]
+    bits = [2**b for b in range(parts.bit_length() - 1)]
+    others = [sum(lax.rem(me // b + k // b, 2) * b for b in bits) for k in range(parts)]
 
     @pl.when(section == 0)
     def _():

time: 21.8 us -> 22.8 us (1.046)
  Pallas kernels: 21.1 us -> 22 us
    pallas_call x1, Pallas kernels: 20.3 us -> 21.2 us  [kernel_per_device(): pl.pallas_call(functools.partial(correlate_kernel, pipes, parts), out_sha...]
where the time goes in v11:
time: 22.8 us; the launch traced here: 22.6 us
  Pallas kernels  22 us (96%)
  between operations  0.64 us (3%)
    pallas_call x1, Pallas kernels, kernel_per_device(): pl.pallas_call(functools.partial(correlate_kernel, pipes, parts), out_sha...  21.2 us
    pallas_call x1, Pallas kernels, kernel_per_device(): pl.pallas_call(finish_kernel, out_shape=(jax.ShapeDtypeStruct((rows, widt...  0.79 us

profile of v11, /device:TPU:0, one launch (start us, length us, event | category | flops | bytes accessed | tf_op | source)
XLA Modules:
  0.0 22.6 jit_solution(5680778713937876582)
XLA Ops:
  0.6 21.2 %shard_map.68.r_ref = bf16[8,2,48,128]{3,2,1,0:T(8,128)(2,1)S(1)} custom-call(bf16[128,256]{1,0:T(8,128)(2,1)} %bitcast.6, f32[128,256]{1,0:T(8,128)} %bitcast.5, f32[1,256]{1,0:T(1,128)} %skip_hbm.1, bf16[128,256]{1,0:T(8,128)(2,1)} %bitcast.7, bf16[128,256]{1,0:T(8,128)(2,1)} %loss_hbm.1), custom_call_target="tpu_custom_call" | custom-call | tf_op jit(solution)/shard_map/pallas_call | solution.py:335
  21.8 0.8 %shard_map.69 = (bf16[128,256]{1,0:T(8,128)(2,1)}, f32[128,256]{1,0:T(8,128)}) custom-call(bf16[8,2,48,128]{3,2,1,0:T(8,128)(2,1)S(1)} %shard_map.68.r_ref), custom_call_target="tpu_custom_call" | custom-call | tf_op jit(solution)/shard_map/pallas_call | solution.py:361
